TPU v7x, 32 devices: a whole 2x2x4 slice. The times are simulated.
32 devices in a mesh: groups: 2 (over y), seq: 4 (over z), dp: 2 (over x), mp: 2 (over core).
Axes of the slice: x: 2, y: 2, z: 4, core: 2. Of those that a mesh axis runs over, the one named last changes fastest.
Arguments:
- features: bfloat16 [4, 16, 144, 1152], P(('groups', 'dp'), 'seq'), parts along dimension 0, may hold values from -6 to 6
- hidden_grad: bfloat16 [4, 256, 4, 1792], P(('groups', 'dp'), None, 'seq', 'mp'), parts along dimension 0, may hold values from -6 to 6
- weight: bfloat16 [1152, 1792], P(None, 'mp'), may hold values from -0.1875 to 0.1875
- bias: float32 [1792], P('mp'), may hold values from -4 to 4
- keep_count: int32 [4, 16], P(('groups', 'dp')), parts along dimension 0, may hold values from 1 to 144, as said below
- keep_order: int32 [4, 16, 144], P(('groups', 'dp'), 'seq'), parts along dimension 0, may hold values from 0 to 143, each once within a row
Outputs:
- grad_features: bfloat16 [4, 16, 144, 1152], P(('groups', 'dp'), 'seq', None, 'mp'), parts along dimension 0
- grad_weight: float32 [2304, 1792], P(('groups', 'seq', 'dp'), 'mp'), parts along dimension 0
There are 2 independent parts, one for each index of `groups`. A program takes and returns all parts, laid end to end along the dimension named above; an argument that names none is the same for every part. Nothing has to cross between parts.
Inputs may be any that keep to these rules, and one draw needn't show every extreme that they name: `keep_count`: every frame keeps at least one token; a video keeps 1024 tokens in all; the 4 frames of one index of seq keep at most 576 tokens, and in every video one index of seq keeps exactly that many. `keep_order`: each frame's row is a permutation of 0 to 143.
All inputs are finite; a program needn't handle non-finite values.
Results may differ from a plain program's by a relative error of at most 0.0049.
Values may be sent and summed in bfloat16 or wider, within the bound.
No kernel may reach another device: no remote copies, remote signals or barrier semaphores. Data moves between devices by JAX's collectives and lax.ppermute only.
A program may use at most 64 MiB of HBM per device.

v0:
```python
import math

import jax
import jax.numpy as jnp
from jax import lax
from jax.sharding import PartitionSpec as P

inv_root_two = 0.7071067811865476
inv_root_tau = 0.3989422804014327


def swapped(array, axis, distance):
    return lax.ppermute(array, axis, [(i, i ^ 1 << distance) for i in range(lax.axis_size(axis))])


def gelu_slope(preact):
    return (
        0.5 * (1.0 + lax.erf(preact * inv_root_two))
        + preact * jnp.exp(-0.5 * preact * preact) * inv_root_tau
    )


def layout(keep_count, seq_size, frames_dev):
    counts = keep_count[0]
    frame_start = jnp.cumsum(counts) - counts
    device_total = counts.reshape(seq_size, frames_dev).sum(axis=1)
    device_start = jnp.cumsum(device_total) - device_total
    return (frame_start, device_start, device_start + device_total)


def encoder_index(my_seq, frame_start, device_start, device_end, keep_order, seq_size, slot_rows):
    frames_dev = keep_order.shape[1]
    patch_count = keep_order.shape[2]
    source = jnp.arange(seq_size, dtype=jnp.int32)[:, None]
    offset = jnp.arange(slot_rows, dtype=jnp.int32)[None, :]
    range_begin = device_start[my_seq]
    finish = device_end[my_seq]
    first_row = (range_begin - source + seq_size - 1) // seq_size
    position = (first_row + offset) * seq_size + source
    live_mask = position < finish
    local_pos = jnp.where(live_mask, position - range_begin, 0)
    local_start = (
        lax.dynamic_slice_in_dim(frame_start, my_seq * frames_dev, frames_dev) - range_begin
    )
    frame_local = jnp.sum((local_pos[..., None] >= local_start).astype(jnp.int32), axis=-1) - 1
    within = local_pos - jnp.take(local_start, frame_local)
    token_id = keep_order[0][frame_local, within]
    dense_index = jnp.where(
        live_mask, frame_local * patch_count + token_id, frames_dev * patch_count
    )
    return (dense_index.reshape(-1), live_mask.reshape(-1))


def shard_rows(my_seq, device_start, device_end, seq_size, slot_rows):
    offset = jnp.arange(slot_rows, dtype=jnp.int32)[None, :]
    first_row = (device_start[:, None] - my_seq + seq_size - 1) // seq_size
    llm_row = first_row + offset
    live_mask = llm_row * seq_size + my_seq < device_end[:, None]
    llm_row = jnp.where(live_mask, llm_row, 0)
    return (llm_row.reshape(-1), live_mask.reshape(-1))


def swap_halves(row_part):
    my_half = lax.axis_index("mp")
    half_width = row_part.shape[1] // 2
    own_part = lax.dynamic_slice_in_dim(row_part, my_half * half_width, half_width, 1)
    peer_part = lax.dynamic_slice_in_dim(row_part, (1 - my_half) * half_width, half_width, 1)
    return own_part + swapped(peer_part, "mp", 0)


def backward(token_rows, grad_rows, weight, bias):
    preact = jnp.dot(token_rows, weight, preferred_element_type=jnp.float32) + bias
    slope_grad = (grad_rows.astype(jnp.float32) * gelu_slope(preact)).astype(jnp.bfloat16)
    weight_part = lax.dot_general(
        token_rows, slope_grad, (((0,), (0,)), ((), ())), preferred_element_type=jnp.float32
    )
    row_part = lax.dot_general(
        slope_grad, weight, (((1,), (1,)), ((), ())), preferred_element_type=jnp.float32
    )
    return (swap_halves(row_part).astype(jnp.bfloat16), slope_grad, weight_part)


def shards(features, hidden_grad, weight, bias, keep_count, keep_order):
    seq_size = lax.axis_size("seq")
    my_seq = lax.axis_index("seq")
    frames_dev = features.shape[1]
    patch_count = features.shape[2]
    model_width = features.shape[3]
    rows_dev = hidden_grad.shape[1]
    slot_rows = (frames_dev * patch_count + seq_size - 1) // seq_size
    frame_start, device_start, device_end = layout(keep_count, seq_size, frames_dev)
    dense_index, dense_live = encoder_index(
        my_seq, frame_start, device_start, device_end, keep_order, seq_size, slot_rows
    )
    llm_row, llm_live = shard_rows(my_seq, device_start, device_end, seq_size, slot_rows)
    flat_tokens = features[0].reshape(frames_dev * patch_count, model_width)
    clipped = jnp.minimum(dense_index, frames_dev * patch_count - 1)
    local_grads = hidden_grad[0, :, 0, :]
    outgoing = jnp.where(llm_live[:, None], local_grads[llm_row], jnp.zeros((), local_grads.dtype))
    grad_rows = lax.all_to_all(outgoing, "seq", split_axis=0, concat_axis=0, tiled=True)
    token_rows = flat_tokens[clipped]
    half_sum, slope_grad, weight_part = backward(token_rows, grad_rows, weight, bias)
    grid = jnp.zeros((frames_dev * patch_count, half_sum.shape[1]), half_sum.dtype)
    grid = grid.at[dense_index].add(half_sum, mode="drop")
    grad_features = grid.reshape(1, frames_dev, patch_count, half_sum.shape[1])
    videos = lax.axis_size("dp")
    norm_scale = 1.0 / math.sqrt(videos * seq_size * rows_dev)
    summed = lax.psum_scatter(weight_part, ("seq", "dp"), scatter_dimension=0, tiled=True)
    return (grad_features, summed * norm_scale)


def solution(mesh):
    return jax.shard_map(
        shards,
        mesh=mesh,
        in_specs=(
            P(("groups", "dp"), "seq", None, None),
            P(("groups", "dp"), None, "seq", "mp"),
            P(None, "mp"),
            P("mp"),
            P(("groups", "dp"), None),
            P(("groups", "dp"), "seq", None),
        ),
        out_specs=(P(("groups", "dp"), "seq", None, "mp"), P(("groups", "seq", "dp"), "mp")),
        check_vma=False,
    )
```

profile of v0, /device:TPU:0, one launch (start us, length us, event | category | flops | bytes accessed | tf_op | source)
XLA Modules:
  0.0 151.1 jit_solution(5282915149742882540)
XLA Ops:
  7.2 0.0 copy-start
  7.2 0.5 broadcast.538
  7.7 1.4 reduce.10
  9.1 0.1 reshape_squeeze.6
  9.2 0.1 reduce_sum.18
  9.3 0.2 broadcast_in_dim.49
  9.5 0.1 iota_add_fusion
  9.6 0.1 add_compare_fusion
  9.7 0.1 add.343
  9.8 0.1 lt.141
  9.8 0.1 lt.143
  10.0 4.8 %gather_fusion.2 = bf16[576,896]{1,0:T(8,128)(2,1)S(1)} fusion(bf16[256,896]{1,0:T(8,128)(2,1)} %bitcast.35, s32[1024]{0:T(1024)S(1)} %pad_clamp_fusion.1), kind=kCustom, calls=%fused_computation.2 | custom fusion | bytes 2066688 | tf_op jit(solution)/shard_map/gather | solution.py:99
  14.8 0.0 copy-start.5
  14.8 1.2 broadcast_select_fusion
  16.0 6.3 %all-to-all-start = ((bf16[4,144,896]{2,1,0:T(8,128)(2,1)}), bf16[4,144,896]{2,1,0:T(8,128)(2,1)}, u32[]{:S(2)}, u32[]{:S(2)}) async-start(bf16[4,144,896]{2,1,0:T(8,128)(2,1)} %broadcast_select_fusion), calls=%async_computation | async-start | bytes 2064384 | tf_op jit(solution)/shard_map/all_to_all | solution.py:100
  22.3 0.1 copy.10
  22.4 0.1 reduce.1
  22.5 0.6 constant_dynamic-slice_fusion.1
  23.1 0.6 dynamic_slice.15
  23.7 0.7 and_select_fusion.1
  24.4 1.4 subtract_select_fusion
  25.8 0.1 convert_reduce_fusion
  25.9 0.1 reshape.457
  26.0 0.0 copy-start.1
  26.0 3.8 %gather_fusion = s32[576]{0:T(1024)S(1)} fusion(s32[4]{0:T(128)S(1)} %get-tuple-element.7, s32[1024]{0:T(1024)S(1)} %pad_clamp_fusion.2), kind=kCustom, calls=%fused_computation | custom fusion | bytes 6912 | tf_op jit(solution)/shard_map/jit(_take)/gather | solution.py:46
  29.8 0.1 gather.18
  29.9 1.4 fusion.10
  31.2 0.1 reshape.463
  31.3 0.0 copy-done.1
  31.3 5.2 %gather_fusion.1 = s32[576]{0:T(1024)S(1)} fusion(s32[4,144]{1,0:T(4,128)S(1)} %bitcast.34, s32[576]{0:T(1024)S(1)} %reshape.463), kind=kCustom, calls=%fused_computation.1 | custom fusion | bytes 9216 | tf_op jit(solution)/shard_map/gather | solution.py:47
  36.6 0.1 reshape.466
  36.6 0.7 add_select_fusion
  37.4 0.1 reshape.453
  37.5 0.0 copy-start.6
  37.5 3.5 %gather_fusion.3 = bf16[576,1152]{1,0:T(8,128)(2,1)} fusion(bf16[576,1152]{1,0:T(8,128)(2,1)S(1)} %bitcast.36, s32[1024]{0:T(1024)S(1)} %pad_clamp_fusion), kind=kCustom, calls=%fused_computation.3 | custom fusion | bytes 2656512 | tf_op jit(solution)/shard_map/gather | solution.py:101
  41.0 6.7 %all-to-all-done = bf16[4,144,896]{2,1,0:T(8,128)(2,1)} async-done(((bf16[4,144,896]{2,1,0:T(8,128)(2,1)}), bf16[4,144,896]{2,1,0:T(8,128)(2,1)}, u32[]{:S(2)}, u32[]{:S(2)}) %all-to-all-start) | async-done | bytes 1032224 | tf_op jit(solution)/shard_map/all_to_all | solution.py:100
  47.8 3.9 %fusion.5 = bf16[576,896]{1,0:T(8,128)(2,1)S(1)} fusion(bf16[576,896]{1,0:T(8,128)(2,1)} %bitcast.14, bf16[576,1152]{1,0:T(8,128)(2,1)} %gather_fusion.3, bf16[1152,896]{1,0:T(8,128)(2,1)S(1)} %copy-done, f32[896]{0:T(1024)S(1)} %copy-done.6), kind=kOutput, calls=%fused_computation.11 | convolution fusion | flops 1195278336 | bytes 5459456 | tf_op jit(solution)/shard_map/dot_general | solution.py:72
  51.6 0.0 copy-done.4
  51.7 3.9 %fusion.17 = f32[1152,896]{1,0:T(8,128)} fusion(bf16[576,1152]{1,0:T(8,128)(2,1)S(1)} %copy-done.4, bf16[576,896]{1,0:T(8,128)(2,1)S(1)} %fusion.5), kind=kOutput, calls=%fused_computation.55 | convolution fusion | flops 1189085184 | bytes 6488064 | tf_op jit(solution)/shard_map/dot_general | solution.py:74
  55.6 0.0 reduce-scatter.2.cloned.1.call-update
  55.6 1.7 %fusion.16 = f32[576,1152]{1,0:T(8,128)S(1)} fusion(bf16[576,896]{1,0:T(8,128)(2,1)S(1)} %fusion.5, bf16[1152,896]{1,0:T(8,128)(2,1)S(1)} %copy-done), kind=kOutput, calls=%fused_computation.54 | convolution fusion | flops 1189085184 | bytes 5750784 | tf_op jit(solution)/shard_map/dot_general | solution.py:77
  57.3 1.5 %copy-done.3 = f32[576,1152]{1,0:T(8,128)} copy-done((f32[576,1152]{1,0:T(8,128)}, f32[576,1152]{1,0:T(8,128)S(1)}, u32[]{:S(2)}) %copy-start.3) | copy-done | bytes 2654232
  58.8 0.4 constant_dynamic-slice_fusion
  59.3 0.1 collective-permute-start
  59.4 3.4 %collective-permute-done = f32[576,576]{1,0:T(8,128)} collective-permute-done((f32[576,576]{1,0:T(8,128)S(1)}, f32[576,576]{1,0:T(8,128)}, u32[]{:S(2)}, u32[]{:S(2)}) %collective-permute-start) | collective-permute-done | bytes 1327136 | tf_op jit(solution)/shard_map/ppermute | solution.py:13
  62.8 10.2 %scatter_custom_fusion = bf16[576,576]{1,0:T(8,128)(2,1)} fusion(s32[576]{0:T(1024)S(1)} %get-tuple-element.3, f32[576,576]{1,0:T(8,128)} %collective-permute-done, f32[576,1152]{1,0:T(8,128)} %copy-done.3, s32[]{:T(128)} %constant.40.clone.1, s32[]{:T(128)S(6)} %select_n.163, bf16[]{:T(256)} %constant.39.clone.1), kind=kCustom, calls=%fused_computation.14 | custom fusion | flops 995328 | bytes 3613700 | tf_op jit(solution)/shard_map/scatter-add | solution.py:104
  72.9 69.5 %reduce-scatter.2.cloned.1.call-done = f32[144,896]{1,0:T(8,128)} async-done(((f32[1152,896]{1,0:T(8,128)}), f32[144,896]{1,0:T(8,128)}) %reduce-scatter.2.cloned.1.call-update) | async-done | bytes 516112 | tf_op jit(solution)/shard_map/reduce_scatter | solution.py:108
  142.4 1.9 %broadcast_multiply_fusion = f32[144,896]{1,0:T(8,128)} fusion(f32[144,896]{1,0:T(8,128)} %reduce-scatter.2.cloned.1.call-done), kind=kLoop, calls=%fused_computation.16 | loop fusion | flops 129024 | bytes 1032192 | tf_op jit(solution)/shard_map/mul | solution.py:109
  (17 shorter events, 0.1 us)
Async XLA Ops:
  7.2 40.6 %copy-start = (bf16[1152,896]{1,0:T(8,128)(2,1)S(1)}, bf16[1152,896]{1,0:T(8,128)(2,1)}, u32[]{:S(2)}) copy-start(bf16[1152,896]{1,0:T(8,128)(2,1)} %param.8) | copy-start | bytes 6193156
  14.8 7.5 %copy-start.5 = (s32[1,16]{1,0:T(1,128)S(1)}, s32[1,16]{1,0:T(1,128)}, u32[]{:S(2)}) copy-start(s32[1,16]{1,0:T(1,128)} %param.10) | copy-start | bytes 196
  16.0 31.8 %all-to-all-start = ((bf16[4,144,896]{2,1,0:T(8,128)(2,1)}), bf16[4,144,896]{2,1,0:T(8,128)(2,1)}, u32[]{:S(2)}, u32[]{:S(2)}) async-start(bf16[4,144,896]{2,1,0:T(8,128)(2,1)} %broadcast_select_fusion), calls=%async_computation | async-start | bytes 2064384 | tf_op jit(solution)/shard_map/all_to_all | solution.py:100
  22.3 120.1 %reduce-scatter.2.cloned.1.call-start = ((), (), s32[]{:S(2)}) async-start(), calls=%async_computation.2 | async-start | bytes 4644864 | tf_op jit(solution)/shard_map/reduce_scatter | solution.py:108
  26.0 5.4 %copy-start.1 = (s32[1,4,144]{2,1,0:T(4,128)S(1)}, s32[1,4,144]{2,1,0:T(4,128)}, u32[]{:S(2)}) copy-start(s32[1,4,144]{2,1,0:T(4,128)} %param.11) | copy-start | bytes 6916
  31.3 6.2 %copy-start.2 = (bf16[1,4,144,1152]{3,2,1,0:T(8,128)(2,1)S(1)}, bf16[1,4,144,1152]{3,2,1,0:T(8,128)(2,1)}, u32[]{:S(2)}) copy-start(bf16[1,4,144,1152]{3,2,1,0:T(8,128)(2,1)} %param.6) | copy-start | bytes 3981316
  37.5 10.2 %copy-start.6 = (f32[896]{0:T(1024)S(1)}, f32[896]{0:T(1024)}, u32[]{:S(2)}) copy-start(f32[896]{0:T(1024)} %param.9) | copy-start | bytes 10756
  47.8 3.9 %copy-start.4 = (bf16[576,1152]{1,0:T(8,128)(2,1)S(1)}, bf16[576,1152]{1,0:T(8,128)(2,1)}, u32[]{:S(2)}) copy-start(bf16[576,1152]{1,0:T(8,128)(2,1)} %gather_fusion.3) | copy-start | bytes 3981316
  57.3 1.5 %copy-start.3 = (f32[576,1152]{1,0:T(8,128)}, f32[576,1152]{1,0:T(8,128)S(1)}, u32[]{:S(2)}) copy-start(f32[576,1152]{1,0:T(8,128)S(1)} %fusion.16) | copy-start | bytes 7962628
  59.3 3.5 %collective-permute-start = (f32[576,576]{1,0:T(8,128)S(1)}, f32[576,576]{1,0:T(8,128)}, u32[]{:S(2)}, u32[]{:S(2)}) collective-permute-start(f32[576,576]{1,0:T(8,128)S(1)} %constant_dynamic-slice_fusion), channel_id=1, source_target_pairs={{0,1},{1,0},{2,3},{3,2},{4,5},{5,4},{6,7},{7,6},{8,9},{9,8},{10,11... | collective-permute-start | bytes 3981320 | tf_op jit(solution)/shard_map/ppermute | solution.py:13
Sparse Core Ops, SparseCore 0:
  55.7 86.6 reduce-scatter.1
where the time goes:
time: 151 us
  waiting for transfers between devices  79.6 us (53%)
  local copies, waits for them, and re-layouts  21.8 us (14%)
  other arithmetic  19.6 us (13%)
  between operations  14.2 us (9%)
  matrix products  9.5 us (6%)
  starting transfers between devices  6.39 us (4%)
    reduce_scatter x1, waiting for transfers between devices, shards(): lax.psum_scatter(weight_part, ('seq', 'dp'), scatter_dimension=0, tiled=T...  69.5 us
    scatter-add x1, other arithmetic, shards(): grid = grid.at[dense_index].add(half_sum, mode='drop')  10.2 us
    all_to_all x1, waiting for transfers between devices, shards(): lax.all_to_all(outgoing, 'seq', split_axis=0, concat_axis=0, tiled=True)  6.74 us
    all_to_all x1, starting transfers between devices, shards(): lax.all_to_all(outgoing, 'seq', split_axis=0, concat_axis=0, tiled=True)  6.32 us
    gather x2, local copies, waits for them, and re-layouts, encoder_index(): token_id = keep_order[0][frame_local, within]  5.3 us
    gather x1, local copies, waits for them, and re-layouts, shards(): local_grads[llm_row]  4.82 us
    dot_general x1, matrix products, backward(): lax.dot_general(token_rows, slope_grad, (((0,), (0,)), ((), ())), preferr...  3.92 us
    dot_general x1, matrix products, backward(): jnp.dot(token_rows, weight, preferred_element_type=jnp.float32) + bias  3.88 us
  transfers between devices with their start and end apart: 3, of which 3 were waited for; matrix products, arithmetic and copies ran while one was open for 20% of the time, Pallas kernels for 0%

commit v1 on v0

v1 whole, which is shorter than its diff:
```python
import functools
import math

import jax
import jax.numpy as jnp
from jax import lax
from jax.experimental import pallas as pl
from jax.experimental.pallas import tpu as pltpu
from jax.sharding import PartitionSpec as P

inv_root_two = 0.7071067811865476
inv_root_tau = 0.3989422804014327
bf16, f32, i32 = jnp.bfloat16, jnp.float32, jnp.int32
vmem = pl.BlockSpec(memory_space=pltpu.VMEM)
smem = pl.BlockSpec(memory_space=pltpu.SMEM)


def call(body, outs, in_specs, scratch=(), flops=0, moved=0, exps=0):
    return pl.pallas_call(
        body,
        out_shape=outs,
        in_specs=in_specs,
        out_specs=[vmem] * len(outs),
        scratch_shapes=list(scratch),
        compiler_params=pltpu.CompilerParams(vmem_limit_bytes=40 << 20),
        cost_estimate=pl.CostEstimate(flops=flops, bytes_accessed=moved, transcendentals=exps),
    )


def shape(dtype, *extent):
    return jax.ShapeDtypeStruct(extent, dtype)


def exchanged(array, axis, distance):
    return lax.ppermute(array, axis, [(i, i ^ distance) for i in range(lax.axis_size(axis))])


def gelu_slope(preact):
    return (
        0.5 * (1.0 + lax.erf(preact * inv_root_two))
        + preact * jnp.exp(-0.5 * preact * preact) * inv_root_tau
    )


def kept_before(count_ref, frame):
    total = jnp.int32(0)
    for index in range(count_ref.shape[1]):
        total += jnp.where(index < frame, count_ref[0, index], 0)
    return total


def slot_start(range_begin, source, seq_size, rows_dev, slot_rows):
    first_row = lax.div(range_begin - source + (seq_size - 1), jnp.int32(seq_size))
    return jnp.minimum(first_row, rows_dev - slot_rows)


def pack_kernel(seq_size, frames_dev, slot_rows, partner, count_ref, grads_ref, *outs):
    my_seq = lax.axis_index("seq")
    rows_dev = grads_ref.shape[0]
    row = lax.broadcasted_iota(i32, (slot_rows, rows_dev), 0)
    column = lax.broadcasted_iota(i32, (slot_rows, rows_dev), 1)
    for k in range(seq_size):
        target = partner(my_seq, k)
        start = slot_start(kept_before(count_ref, target * frames_dev), my_seq, seq_size, rows_dev, slot_rows)
        picks = jnp.where(column == row + start, 1.0, 0.0).astype(bf16)
        rows = jnp.dot(picks, grads_ref[...], preferred_element_type=f32).astype(bf16)
        if len(outs) == 1:
            outs[0][k] = rows
        else:
            outs[k][...] = rows


def slope_kernel(
    seq_size, rows_dev, slot_rows, partner, count_ref, order_ref, tokens_ref, weight_ref, bias_ref,
    slope_ref, rows_t_ref, place_ref, slot_pos, token_pos, rows_ref,
):
    my_seq = lax.axis_index("seq")
    frames_dev, patches = order_ref.shape
    tokens, width = tokens_ref.shape
    slots = slope_ref.shape[0]
    range_begin = kept_before(count_ref, my_seq * frames_dev)
    step = lax.broadcasted_iota(i32, (slot_rows, 1), 0)
    lane = lax.broadcasted_iota(i32, (1, slots), 1)
    slot_row = jnp.zeros((1, slots), i32)
    for k in range(seq_size):
        source = partner(my_seq, k)
        start = slot_start(range_begin, source, seq_size, rows_dev, slot_rows)
        slot_pos[k * slot_rows:(k + 1) * slot_rows, :] = (start + step) * seq_size + source
        slot_row = jnp.where(lane >= k * slot_rows, (start + lane - k * slot_rows) * seq_size + source, slot_row)
    token = lax.broadcasted_iota(i32, (patches, patches), 0)
    index = lax.broadcasted_iota(i32, (patches, patches), 1)
    begin = range_begin
    for frame in range(frames_dev):
        count = count_ref[0, my_seq * frames_dev + frame]
        order = order_ref[frame:frame + 1, :]
        rank = jnp.sum(jnp.where(order == token, index, 0), axis=1, keepdims=True)
        token_pos[frame * patches:(frame + 1) * patches, :] = jnp.where(rank < count, rank + begin, -1)
        begin += count
    column = token_pos[...]
    place_ref[...] = jnp.where(column == slot_row, 1.0, 0.0).astype(bf16)
    row = lax.broadcasted_iota(i32, (tokens, tokens), 0)
    lane = lax.broadcasted_iota(i32, (tokens, tokens), 1)
    token_row = jnp.sum(jnp.where(row == lane, column, 0), axis=0, keepdims=True)
    block = slots // 4

    @pl.loop(0, 4)
    def _(part):
        here = pl.ds(pl.multiple_of(part * block, 16), block)
        picks = jnp.where(slot_pos[here, :] == token_row, 1.0, 0.0).astype(bf16)
        rows = jnp.dot(picks, tokens_ref[...], preferred_element_type=f32).astype(bf16)
        rows_ref[here, :] = rows
        preact = jnp.dot(rows, weight_ref[...], preferred_element_type=f32) + bias_ref[...]
        slope_ref[here, :] = gelu_slope(preact)

    rows_t_ref[...] = rows_ref[...].T


def grad_kernel(chunks, tile, slots_in, *refs):
    grads, (slope_ref, rows_t_ref, grad_ref), outs = refs[:slots_in], refs[slots_in:slots_in + 3], refs[slots_in + 3:]
    slot_rows = grads[0].shape[0]
    for k, ref in enumerate(grads):
        here = slice(k * slot_rows, (k + 1) * slot_rows)
        grad_ref[here, :] = (ref[...].astype(f32) * slope_ref[here, :]).astype(bf16)
    weight_tiles(chunks, tile, rows_t_ref, grad_ref, outs)


def weight_tiles(chunks, tile, rows_t_ref, grad_ref, outs):
    my_seq, my_dp = lax.axis_index("seq"), lax.axis_index("dp")
    videos = lax.axis_size("dp")
    for (k, j), ref in zip(chunks, outs):
        owner = (my_seq ^ k) * videos + (my_dp ^ j)
        rows = rows_t_ref[pl.ds(pl.multiple_of(owner * tile, 16), tile), :]
        ref[...] = jnp.dot(rows, grad_ref[...], preferred_element_type=f32).astype(ref.dtype)


def tiles_kernel(chunks, tile, rows_t_ref, grad_ref, *outs):
    weight_tiles(chunks, tile, rows_t_ref, grad_ref, outs)


def row_kernel(grad_ref, weight_ref, own_ref, peer_ref):
    my_half = lax.axis_index("mp")
    half = own_ref.shape[1]
    for ref, which in ((peer_ref, 1 - my_half), (own_ref, my_half)):
        part = weight_ref[pl.ds(pl.multiple_of(which * half, 16), half), :]
        ref[...] = lax.dot_general(grad_ref[...], part, (((1,), (1,)), ((), ())), preferred_element_type=f32)


def place_kernel(own_ref, peer_ref, place_ref, out_ref):
    rows = (own_ref[...] + peer_ref[...]).astype(bf16)
    out_ref[...] = jnp.dot(place_ref[...], rows, preferred_element_type=f32).astype(bf16)


def shards(features, hidden_grad, weight, bias, keep_count, keep_order):
    seq_size, videos = lax.axis_size("seq"), lax.axis_size("dp")
    frames_dev, patches, width = features.shape[1:]
    rows_dev, hidden = hidden_grad.shape[1], hidden_grad.shape[3]
    tokens = frames_dev * patches
    slot_rows = (tokens + seq_size - 1) // seq_size
    slot_rows = (slot_rows + 15) // 16 * 16
    slots = seq_size * slot_rows
    tile = width // (seq_size * videos)
    direct = seq_size <= 8 and videos <= 2 and tile % 16 == 0
    norm_scale = 1.0 / math.sqrt(videos * seq_size * rows_dev)

    def partner(me, k):
        return me ^ k if direct else jnp.int32(k)

    local_grads = hidden_grad.reshape(rows_dev, hidden)
    flat_tokens = features.reshape(tokens, width)
    one = shape(bf16, slot_rows, hidden)
    outgoing = call(
        functools.partial(pack_kernel, seq_size, frames_dev, slot_rows, partner),
        [one] * seq_size if direct else [shape(bf16, seq_size, slot_rows, hidden)],
        [smem, vmem],
        flops=2 * slots * rows_dev * hidden,
        moved=2 * hidden * (rows_dev + slots),
    )(keep_count, local_grads)
    if direct:
        arrived = [exchanged(rows, "seq", k) if k else rows for k, rows in enumerate(outgoing)]
    else:
        arrived = [lax.all_to_all(outgoing[0], "seq", split_axis=0, concat_axis=0, tiled=True).reshape(slots, hidden)]

    slope, rows_t, place = call(
        functools.partial(slope_kernel, seq_size, rows_dev, slot_rows, partner),
        [shape(f32, slots, hidden), shape(bf16, width, slots), shape(bf16, tokens, slots)],
        [smem, vmem, vmem, vmem, vmem],
        [pltpu.VMEM((slots, 1), i32), pltpu.VMEM((tokens, 1), i32), pltpu.VMEM((slots, width), bf16)],
        flops=2 * slots * width * (tokens + hidden),
        moved=2 * width * (tokens + hidden + slots) + 4 * slots * hidden,
        exps=2 * slots * hidden,
    )(keep_count, keep_order.reshape(frames_dev, patches), flat_tokens, weight, bias.reshape(1, hidden))

    order = [k for k in range(seq_size - 1, -1, -1)]
    sent = [(k, 1) for k in order] if direct and videos == 2 else []
    own = [(k, 0) for k in order] if direct else []
    tile_flops, tile_bytes = 2 * tile * slots * hidden, 4 * tile * hidden
    slope_grad, *first = call(
        functools.partial(grad_kernel, sent[:1], tile, len(arrived)),
        [shape(bf16, slots, hidden)] + [shape(bf16, tile, hidden)] * len(sent[:1]),
        [vmem] * (len(arrived) + 2),
        flops=tile_flops,
        moved=8 * slots * hidden + 2 * slots * width,
    )(*arrived, slope, rows_t)
    if direct:
        rest = call(
            functools.partial(tiles_kernel, sent[1:], tile),
            [shape(bf16, tile, hidden)] * len(sent[1:]),
            [vmem, vmem],
            flops=tile_flops * len(sent[1:]),
            moved=tile_bytes * len(sent[1:]),
        )(rows_t, slope_grad) if sent[1:] else []
        mine = call(
            functools.partial(tiles_kernel, own, tile),
            [shape(f32, tile, hidden)] * len(own),
            [vmem, vmem],
            flops=tile_flops * len(own),
            moved=tile_bytes * len(own),
        )(rows_t, slope_grad)
        from_dp = [exchanged(part, "dp", 1) for part in first + list(rest)]
        sums = [part + peer.astype(f32) for part, peer in zip(mine, from_dp)] if sent else mine
        summed = sums[-1]
        for k, part in zip(order[:-1], sums[:-1]):
            summed = summed + exchanged(part.astype(bf16), "seq", k).astype(f32)
    else:
        partial = jnp.dot(rows_t, slope_grad, preferred_element_type=f32)
        summed = lax.psum_scatter(partial, ("seq", "dp"), scatter_dimension=0, tiled=True)

    half = width // lax.axis_size("mp")
    own_part, peer_part = call(
        row_kernel,
        [shape(f32, slots, half)] * 2,
        [vmem, vmem],
        flops=2 * slots * width * hidden,
        moved=2 * hidden * (slots + width) + 4 * slots * width,
    )(slope_grad, weight)
    peer_part = exchanged(peer_part, "mp", 1)
    (grid,) = call(
        place_kernel,
        [shape(bf16, tokens, half)],
        [vmem] * 3,
        flops=2 * tokens * slots * half,
        moved=2 * tokens * (slots + half) + 8 * slots * half,
    )(own_part, peer_part, place)
    return (grid.reshape(1, frames_dev, patches, half), summed * norm_scale)


def solution(mesh):
    return jax.shard_map(
        shards,
        mesh=mesh,
        in_specs=(
            P(("groups", "dp"), "seq", None, None),
            P(("groups", "dp"), None, "seq", "mp"),
            P(None, "mp"),
            P("mp"),
            P(("groups", "dp"), None),
            P(("groups", "dp"), "seq", None),
        ),
        out_specs=(P(("groups", "dp"), "seq", None, "mp"), P(("groups", "seq", "dp"), "mp")),
        check_vma=False,
    )
```

time: 151 us -> 69 us (0.46)
  waiting for transfers between devices: 79.6 us -> 22.1 us
  starting transfers between devices: 6.39 us -> 26.4 us
  other arithmetic: 19.6 us -> 1.13 us
  local copies, waits for them, and re-layouts: 21.8 us -> 5.95 us
  between operations: 14.2 us -> 0.73 us
  Pallas kernels: 0 us -> 12.4 us
  matrix products: 9.5 us -> 0 us
    reduce_scatter x1 -> x0, waiting for transfers between devices: 69.5 us -> none  [shards(): lax.psum_scatter(weight_part, ('seq', 'dp'), scatter_dimension=0, tiled=T...]
    ppermute x1 -> x11, starting transfers between devices: 0.07 us -> 26.4 us  [exchanged(): lax.ppermute(array, axis, [(i, i ^ distance) for i in range(lax.axis_size...]
    ppermute x1 -> x11, waiting for transfers between devices: 3.38 us -> 22.1 us  [exchanged(): lax.ppermute(array, axis, [(i, i ^ distance) for i in range(lax.axis_size...]
    gather x6 -> x0, local copies, waits for them, and re-layouts: 17.5 us -> none  [the longest x2 5.3 us: encoder_index(): token_id = keep_order[0][frame_local, within]]
    pallas_call x0 -> x7, Pallas kernels: none -> 12.4 us  [the longest x1 5.23 us: shards(): call(functools.partial(slope_kernel, seq_size, rows_dev, slot_rows, partn...]
    scatter-add x1 -> x0, other arithmetic: 10.2 us -> none  [shards(): grid = grid.at[dense_index].add(half_sum, mode='drop')]
    dot_general x3 -> x0, matrix products: 9.5 us -> none  [the longest x1 3.92 us: backward(): lax.dot_general(token_rows, slope_grad, (((0,), (0,)), ((), ())), preferr...]
    all_to_all x1 -> x0, waiting for transfers between devices: 6.74 us -> none  [shards(): lax.all_to_all(outgoing, 'seq', split_axis=0, concat_axis=0, tiled=True)]
  transfers between devices with their start and end apart: 3 -> 11, of which waited for: 3 -> 5; matrix products, arithmetic and copies ran while one was open for 20% -> 3% of each run, Pallas kernels for 0% -> 13%
where the time goes in v1:
time: 69 us; the launch traced here: 68.7 us
  starting transfers between devices  26.4 us (38%)
  waiting for transfers between devices  22.1 us (32%)
  Pallas kernels  12.4 us (18%)
  local copies, waits for them, and re-layouts  5.95 us (9%)
  other arithmetic  1.13 us (2%)
  between operations  0.73 us (1%)
    ppermute x11, starting transfers between devices, exchanged(): lax.ppermute(array, axis, [(i, i ^ distance) for i in range(lax.axis_size...  26.4 us
    ppermute x11, waiting for transfers between devices, exchanged(): lax.ppermute(array, axis, [(i, i ^ distance) for i in range(lax.axis_size...  22.1 us
    unnamed x12, local copies, waits for them, and re-layouts  5.26 us
    pallas_call x1, Pallas kernels, shards(): call(functools.partial(slope_kernel, seq_size, rows_dev, slot_rows, partn...  5.23 us
    pallas_call x1, Pallas kernels, shards(): call(row_kernel, [shape(f32, slots, half)] * 2, [vmem, vmem], flops=2 * s...  1.95 us
    pallas_call x1, Pallas kernels, shards(): call(place_kernel, [shape(bf16, tokens, half)], [vmem] * 3, flops=2 * tok...  1.71 us
  transfers between devices with their start and end apart: 11, of which 5 were waited for; matrix products, arithmetic and copies ran while one was open for 3% of the time, Pallas kernels for 13%

profile of v1, /device:TPU:0, one launch (start us, length us, event | category | flops | bytes accessed | tf_op | source)
XLA Modules:
  0.0 68.7 jit_solution(4930106220781162531)
XLA Ops:
  0.6 0.0 copy-start.3
  0.6 1.0 %copy-done.3 = bf16[1,256,1,896]{3,1,2,0:T(8,128)(2,1)S(1)} copy-done((bf16[1,256,1,896]{3,1,2,0:T(8,128)(2,1)S(1)}, bf16[1,256,1,896]{3,1,2,0:T(8,128)(2,1)}, u32[]{:S(2)}) %copy-start.3) | copy-done | bytes 458776
  1.6 0.0 copy-start.5
  1.7 0.7 copy-done.5
  2.3 1.0 %shard_map.77 = (bf16[144,896]{1,0:T(8,128)(2,1)S(1)}, bf16[144,896]{1,0:T(8,128)(2,1)S(1)}, bf16[144,896]{1,0:T(8,128)(2,1)S(1)}, bf16[144,896]{1,0:T(8,128)(2,1)S(1)}) custom-call(s32[1,16]{1,0:T(1,128)S(1)} %copy-done.5, bf16[256,896]{1,0:T(8,128)(2,1)S(1)} %bitcast.5), custom_call_target="tpu_custom_call" | custom-call | flops 264241152 | bytes 1490944 | tf_op jit(solution)/shard_map/pallas_call | solution.py:171
  3.3 3.1 %collective-permute-start = (bf16[144,896]{1,0:T(8,128)(2,1)S(1)}, bf16[144,896]{1,0:T(8,128)(2,1)S(1)}, u32[]{:S(2)}, u32[]{:S(2)}) collective-permute-start(bf16[144,896]{1,0:T(8,128)(2,1)S(1)} %get-tuple-element.21), channel_id=1, source_target_pairs={{0,4},{4,0},{8,12},{12,8},{1,5},{5,1},{9,13},{13,9},{2,6},{6,2},{1... | collective-permute-start | bytes 774152 | tf_op jit(solution)/shard_map/ppermute | solution.py:35
  6.4 2.6 %collective-permute-start.1 = (bf16[144,896]{1,0:T(8,128)(2,1)S(1)}, bf16[144,896]{1,0:T(8,128)(2,1)S(1)}, u32[]{:S(2)}, u32[]{:S(2)}) collective-permute-start(bf16[144,896]{1,0:T(8,128)(2,1)S(1)} %get-tuple-element.22), channel_id=1, source_target_pairs={{0,8},{4,12},{8,0},{12,4},{1,9},{5,13},{9,1},{13,5},{2,10},{6,14},... | collective-permute-start | bytes 774152 | tf_op jit(solution)/shard_map/ppermute | solution.py:35
  9.0 0.0 collective-permute-start.2
  9.0 0.7 %reshape.22.bias_ref = f32[1,896]{1,0:T(1,128)S(1)} reshape(f32[896]{0:T(1024)} %param.9) | data formatting | bytes 7168 | tf_op jit(solution)/shard_map/reshape | solution.py:191
  9.7 0.0 copy-start
  9.7 1.6 %copy-done = bf16[1152,896]{1,0:T(8,128)(2,1)S(1)} copy-done((bf16[1152,896]{1,0:T(8,128)(2,1)S(1)}, bf16[1152,896]{1,0:T(8,128)(2,1)}, u32[]{:S(2)}) %copy-start) | copy-done | bytes 2064408
  11.3 0.0 copy-start.2
  11.3 1.3 %copy-done.2 = bf16[1,4,144,1152]{3,2,1,0:T(8,128)(2,1)S(1)} copy-done((bf16[1,4,144,1152]{3,2,1,0:T(8,128)(2,1)S(1)}, bf16[1,4,144,1152]{3,2,1,0:T(8,128)(2,1)}, u32[]{:S(2)}) %copy-start.2) | copy-done | bytes 1327128
  12.6 0.0 copy-start.4
  12.6 0.7 copy-done.4
  13.3 5.2 %shard_map.78 = (f32[576,896]{1,0:T(8,128)S(1)}, bf16[1152,576]{1,0:T(8,128)(2,1)S(1)}, bf16[576,576]{1,0:T(8,128)(2,1)S(1)}) custom-call(s32[1,16]{1,0:T(1,128)S(1)} %copy-done.5, s32[4,144]{1,0:T(4,128)S(1)} %bitcast.6, bf16[576,1152]{1,0:T(8,128)(2,1)S(1)} %bitcast.4, bf16[1152,896]{1,0:T(8,128)(2,1)S(1)} %copy-done, f32[1,896]{1,0:T(1,128)S(1)} %reshape.22.bias_ref), custom_call_target="tpu_custom_call" | custom-call | flops 1953497088 | bytes 6782976 | tf_op jit(solution)/shard_map/pallas_call | solution.py:183
  18.5 0.0 collective-permute-done.refs_1_
  18.5 9.0 %collective-permute-done.1.refs_2_ = bf16[144,896]{1,0:T(8,128)(2,1)S(1)} collective-permute-done((bf16[144,896]{1,0:T(8,128)(2,1)S(1)}, bf16[144,896]{1,0:T(8,128)(2,1)S(1)}, u32[]{:S(2)}, u32[]{:S(2)}) %collective-permute-start.1) | collective-permute-done | bytes 258080 | tf_op jit(solution)/shard_map/ppermute | solution.py:35
  27.5 0.0 collective-permute-done.2.refs_3_
  27.5 0.5 shard_map.79
  28.0 0.0 copy-start.1
  28.0 1.6 %collective-permute-start.5 = (bf16[144,896]{1,0:T(8,128)(2,1)S(1)}, bf16[144,896]{1,0:T(8,128)(2,1)S(1)}, u32[]{:S(2)}, u32[]{:S(2)}) collective-permute-start(bf16[144,896]{1,0:T(8,128)(2,1)S(1)} %get-tuple-element.33), channel_id=1, source_target_pairs={{0,2},{2,0},{1,3},{3,1},{4,6},{6,4},{5,7},{7,5},{8,10},{10,8},{9,1... | collective-permute-start | bytes 774152 | tf_op jit(solution)/shard_map/ppermute | solution.py:35
  29.6 0.9 %shard_map.83 = (bf16[144,896]{1,0:T(8,128)(2,1)S(1)}, bf16[144,896]{1,0:T(8,128)(2,1)S(1)}, bf16[144,896]{1,0:T(8,128)(2,1)S(1)}) custom-call(bf16[1152,576]{1,0:T(8,128)(2,1)S(1)} %get-tuple-element.25.refs_5_.rows_t_ref, bf16[576,896]{1,0:T(8,128)(2,1)S(1)} %get-tuple-element.26.grad_ref), custom_call_target="tpu_custom_call" | custom-call | flops 445906944 | bytes 1548288 | tf_op jit(solution)/shard_map/pallas_call | solution.py:205
  30.5 0.6 collective-permute-start.7
  31.1 0.0 copy-done.1
  31.1 1.9 %shard_map.80 = (f32[576,576]{1,0:T(8,128)S(1)}, f32[576,576]{1,0:T(8,128)S(1)}) custom-call(bf16[576,896]{1,0:T(8,128)(2,1)S(1)} %get-tuple-element.26.grad_ref, bf16[1152,896]{1,0:T(8,128)(2,1)S(1)} %copy-done.1), custom_call_target="tpu_custom_call" | custom-call | flops 1189085184 | bytes 5750784 | tf_op jit(solution)/shard_map/pallas_call | solution.py:229
  33.0 0.1 collective-permute-start.3
  33.1 1.1 %shard_map.82 = (f32[144,896]{1,0:T(8,128)S(1)}, f32[144,896]{1,0:T(8,128)S(1)}, f32[144,896]{1,0:T(8,128)S(1)}, f32[144,896]{1,0:T(8,128)S(1)}) custom-call(bf16[1152,576]{1,0:T(8,128)(2,1)S(1)} %get-tuple-element.25.refs_5_.rows_t_ref, bf16[576,896]{1,0:T(8,128)(2,1)S(1)} %get-tuple-element.26.grad_ref), custom_call_target="tpu_custom_call" | custom-call | flops 594542592 | bytes 2064384 | tf_op jit(solution)/shard_map/pallas_call | solution.py:212
  34.2 1.5 %collective-permute-start.4 = (bf16[144,896]{1,0:T(8,128)(2,1)S(1)}, bf16[144,896]{1,0:T(8,128)(2,1)S(1)}, u32[]{:S(2)}, u32[]{:S(2)}) collective-permute-start(bf16[144,896]{1,0:T(8,128)(2,1)S(1)} %get-tuple-element.31), channel_id=1, source_target_pairs={{0,2},{2,0},{1,3},{3,1},{4,6},{6,4},{5,7},{7,5},{8,10},{10,8},{9,1... | collective-permute-start | bytes 774152 | tf_op jit(solution)/shard_map/ppermute | solution.py:35
  35.8 0.6 collective-permute-start.9
  36.3 0.0 collective-permute-done.5
  36.4 0.1 add_convert_fusion.2
  36.4 2.5 %collective-permute-start.6 = (bf16[144,896]{1,0:T(8,128)(2,1)S(1)}, bf16[144,896]{1,0:T(8,128)(2,1)S(1)}, u32[]{:S(2)}, u32[]{:S(2)}) collective-permute-start(bf16[144,896]{1,0:T(8,128)(2,1)S(1)} %add_convert_fusion.2), channel_id=1, source_target_pairs={{0,12},{4,8},{8,4},{12,0},{1,13},{5,9},{9,5},{13,1},{2,14},{6,10},... | collective-permute-start | bytes 774152 | tf_op jit(solution)/shard_map/ppermute | solution.py:35
  38.9 1.8 %collective-permute-done.7 = bf16[144,896]{1,0:T(8,128)(2,1)S(1)} collective-permute-done((bf16[144,896]{1,0:T(8,128)(2,1)S(1)}, bf16[144,896]{1,0:T(8,128)(2,1)S(1)}, u32[]{:S(2)}, u32[]{:S(2)}) %collective-permute-start.7) | collective-permute-done | bytes 258080 | tf_op jit(solution)/shard_map/ppermute | solution.py:35
  40.8 0.1 add_convert_fusion.1
  40.8 7.8 %collective-permute-start.8 = (bf16[144,896]{1,0:T(8,128)(2,1)S(1)}, bf16[144,896]{1,0:T(8,128)(2,1)S(1)}, u32[]{:S(2)}, u32[]{:S(2)}) collective-permute-start(bf16[144,896]{1,0:T(8,128)(2,1)S(1)} %add_convert_fusion.1), channel_id=1, source_target_pairs={{0,8},{4,12},{8,0},{12,4},{1,9},{5,13},{9,1},{13,5},{2,10},{6,14},... | collective-permute-start | bytes 774152 | tf_op jit(solution)/shard_map/ppermute | solution.py:35
  48.6 1.6 %collective-permute-done.9 = bf16[144,896]{1,0:T(8,128)(2,1)S(1)} collective-permute-done((bf16[144,896]{1,0:T(8,128)(2,1)S(1)}, bf16[144,896]{1,0:T(8,128)(2,1)S(1)}, u32[]{:S(2)}, u32[]{:S(2)}) %collective-permute-start.9) | collective-permute-done | bytes 258080 | tf_op jit(solution)/shard_map/ppermute | solution.py:35
  50.2 6.1 %collective-permute-start.10 = (bf16[144,896]{1,0:T(8,128)(2,1)S(1)}, bf16[144,896]{1,0:T(8,128)(2,1)S(1)}, u32[]{:S(2)}, u32[]{:S(2)}) collective-permute-start(bf16[144,896]{1,0:T(8,128)(2,1)S(1)} %add_convert_fusion), channel_id=1, source_target_pairs={{0,4},{4,0},{8,12},{12,8},{1,5},{5,1},{9,13},{13,9},{2,6},{6,2},{1... | collective-permute-start | bytes 774152 | tf_op jit(solution)/shard_map/ppermute | solution.py:35
  56.3 0.0 collective-permute-done.4
  56.3 0.0 collective-permute-done.6
  56.3 6.7 %collective-permute-done.8 = bf16[144,896]{1,0:T(8,128)(2,1)S(1)} collective-permute-done((bf16[144,896]{1,0:T(8,128)(2,1)S(1)}, bf16[144,896]{1,0:T(8,128)(2,1)S(1)}, u32[]{:S(2)}, u32[]{:S(2)}) %collective-permute-start.8) | collective-permute-done | bytes 258080 | tf_op jit(solution)/shard_map/ppermute | solution.py:35
  63.0 3.0 %collective-permute-done.10 = bf16[144,896]{1,0:T(8,128)(2,1)S(1)} collective-permute-done((bf16[144,896]{1,0:T(8,128)(2,1)S(1)}, bf16[144,896]{1,0:T(8,128)(2,1)S(1)}, u32[]{:S(2)}, u32[]{:S(2)}) %collective-permute-start.10) | collective-permute-done | bytes 258080 | tf_op jit(solution)/shard_map/ppermute | solution.py:35
  66.0 1.0 %add_multiply_fusion = f32[144,896]{1,0:T(8,128)} fusion(bf16[144,896]{1,0:T(8,128)(2,1)S(1)} %collective-permute-done.10, bf16[144,896]{1,0:T(8,128)(2,1)S(1)} %collective-permute-done.8, bf16[144,896]{1,0:T(8,128)(2,1)S(1)} %collective-permute-done.6, f32[144,896]{1,0:T(8,128)S(1)} %get-tuple-element.30, bf16[144,896]{1,0:T(8,128)(2,1)S(1)} %collective-permute-done.4), kind=kLoop, calls=%fused_computation | loop fusion | flops 1161216 | bytes 2064384 | tf_op jit(solution)/shard_map/mul | solution.py:244
  66.9 0.0 collective-permute-done.3.peer_ref
  66.9 1.7 %shard_map.81 = bf16[576,576]{1,0:T(8,128)(2,1)} custom-call(f32[576,576]{1,0:T(8,128)S(1)} %get-tuple-element.27.own_ref, f32[576,576]{1,0:T(8,128)S(1)} %collective-permute-done.3.peer_ref, bf16[576,576]{1,0:T(8,128)(2,1)S(1)} %get-tuple-element.29.place_ref), custom_call_target="tpu_custom_call" | custom-call | flops 382205952 | bytes 3981312 | tf_op jit(solution)/shard_map/pallas_call | solution.py:237
  (1 shorter events, 0.0 us)
Async XLA Ops:
  0.6 1.0 %copy-start.3 = (bf16[1,256,1,896]{3,1,2,0:T(8,128)(2,1)S(1)}, bf16[1,256,1,896]{3,1,2,0:T(8,128)(2,1)}, u32[]{:S(2)}) copy-start(bf16[1,256,1,896]{3,1,2,0:T(8,128)(2,1)} %param.7) | copy-start | bytes 1376260
  1.6 0.7 copy-start.5
  3.3 15.2 %collective-permute-start = (bf16[144,896]{1,0:T(8,128)(2,1)S(1)}, bf16[144,896]{1,0:T(8,128)(2,1)S(1)}, u32[]{:S(2)}, u32[]{:S(2)}) collective-permute-start(bf16[144,896]{1,0:T(8,128)(2,1)S(1)} %get-tuple-element.21), channel_id=1, source_target_pairs={{0,4},{4,0},{8,12},{12,8},{1,5},{5,1},{9,13},{13,9},{2,6},{6,2},{1... | collective-permute-start | bytes 774152 | tf_op jit(solution)/shard_map/ppermute | solution.py:35
  6.4 21.1 %collective-permute-start.1 = (bf16[144,896]{1,0:T(8,128)(2,1)S(1)}, bf16[144,896]{1,0:T(8,128)(2,1)S(1)}, u32[]{:S(2)}, u32[]{:S(2)}) collective-permute-start(bf16[144,896]{1,0:T(8,128)(2,1)S(1)} %get-tuple-element.22), channel_id=1, source_target_pairs={{0,8},{4,12},{8,0},{12,4},{1,9},{5,13},{9,1},{13,5},{2,10},{6,14},... | collective-permute-start | bytes 774152 | tf_op jit(solution)/shard_map/ppermute | solution.py:35
  9.0 18.5 %collective-permute-start.2 = (bf16[144,896]{1,0:T(8,128)(2,1)S(1)}, bf16[144,896]{1,0:T(8,128)(2,1)S(1)}, u32[]{:S(2)}, u32[]{:S(2)}) collective-permute-start(bf16[144,896]{1,0:T(8,128)(2,1)S(1)} %get-tuple-element.23), channel_id=1, source_target_pairs={{0,12},{4,8},{8,4},{12,0},{1,13},{5,9},{9,5},{13,1},{2,14},{6,10},... | collective-permute-start | bytes 774152 | tf_op jit(solution)/shard_map/ppermute | solution.py:35
  9.7 1.6 %copy-start = (bf16[1152,896]{1,0:T(8,128)(2,1)S(1)}, bf16[1152,896]{1,0:T(8,128)(2,1)}, u32[]{:S(2)}) copy-start(bf16[1152,896]{1,0:T(8,128)(2,1)} %weight_ref.3) | copy-start | bytes 6193156
  11.3 1.3 %copy-start.2 = (bf16[1,4,144,1152]{3,2,1,0:T(8,128)(2,1)S(1)}, bf16[1,4,144,1152]{3,2,1,0:T(8,128)(2,1)}, u32[]{:S(2)}) copy-start(bf16[1,4,144,1152]{3,2,1,0:T(8,128)(2,1)} %param.6) | copy-start | bytes 3981316
  12.6 0.7 %copy-start.4 = (s32[1,4,144]{2,1,0:T(4,128)S(1)}, s32[1,4,144]{2,1,0:T(4,128)}, u32[]{:S(2)}) copy-start(s32[1,4,144]{2,1,0:T(4,128)} %param.11) | copy-start | bytes 6916
  28.0 3.1 %copy-start.1 = (bf16[1152,896]{1,0:T(8,128)(2,1)S(1)}, bf16[1152,896]{1,0:T(8,128)(2,1)}, u32[]{:S(2)}) copy-start(bf16[1152,896]{1,0:T(8,128)(2,1)} %weight_ref.3) | copy-start | bytes 6193156
  28.0 8.3 %collective-permute-start.5 = (bf16[144,896]{1,0:T(8,128)(2,1)S(1)}, bf16[144,896]{1,0:T(8,128)(2,1)S(1)}, u32[]{:S(2)}, u32[]{:S(2)}) collective-permute-start(bf16[144,896]{1,0:T(8,128)(2,1)S(1)} %get-tuple-element.33), channel_id=1, source_target_pairs={{0,2},{2,0},{1,3},{3,1},{4,6},{6,4},{5,7},{7,5},{8,10},{10,8},{9,1... | collective-permute-start | bytes 774152 | tf_op jit(solution)/shard_map/ppermute | solution.py:35
  30.5 10.3 %collective-permute-start.7 = (bf16[144,896]{1,0:T(8,128)(2,1)S(1)}, bf16[144,896]{1,0:T(8,128)(2,1)S(1)}, u32[]{:S(2)}, u32[]{:S(2)}) collective-permute-start(bf16[144,896]{1,0:T(8,128)(2,1)S(1)} %get-tuple-element.35), channel_id=1, source_target_pairs={{0,2},{2,0},{1,3},{3,1},{4,6},{6,4},{5,7},{7,5},{8,10},{10,8},{9,1... | collective-permute-start | bytes 774152 | tf_op jit(solution)/shard_map/ppermute | solution.py:35
  33.0 33.9 %collective-permute-start.3 = (f32[576,576]{1,0:T(8,128)S(1)}, f32[576,576]{1,0:T(8,128)S(1)}, u32[]{:S(2)}, u32[]{:S(2)}) collective-permute-start(f32[576,576]{1,0:T(8,128)S(1)} %get-tuple-element.28), channel_id=1, source_target_pairs={{0,1},{1,0},{2,3},{3,2},{4,5},{5,4},{6,7},{7,6},{8,9},{9,8},{10,11... | collective-permute-start | bytes 3981320 | tf_op jit(solution)/shard_map/ppermute | solution.py:35
  34.2 22.1 %collective-permute-start.4 = (bf16[144,896]{1,0:T(8,128)(2,1)S(1)}, bf16[144,896]{1,0:T(8,128)(2,1)S(1)}, u32[]{:S(2)}, u32[]{:S(2)}) collective-permute-start(bf16[144,896]{1,0:T(8,128)(2,1)S(1)} %get-tuple-element.31), channel_id=1, source_target_pairs={{0,2},{2,0},{1,3},{3,1},{4,6},{6,4},{5,7},{7,5},{8,10},{10,8},{9,1... | collective-permute-start | bytes 774152 | tf_op jit(solution)/shard_map/ppermute | solution.py:35
  35.8 14.4 %collective-permute-start.9 = (bf16[144,896]{1,0:T(8,128)(2,1)S(1)}, bf16[144,896]{1,0:T(8,128)(2,1)S(1)}, u32[]{:S(2)}, u32[]{:S(2)}) collective-permute-start(bf16[144,896]{1,0:T(8,128)(2,1)S(1)} %get-tuple-element.37), channel_id=1, source_target_pairs={{0,2},{2,0},{1,3},{3,1},{4,6},{6,4},{5,7},{7,5},{8,10},{10,8},{9,1... | collective-permute-start | bytes 774152 | tf_op jit(solution)/shard_map/ppermute | solution.py:35
  36.4 19.9 %collective-permute-start.6 = (bf16[144,896]{1,0:T(8,128)(2,1)S(1)}, bf16[144,896]{1,0:T(8,128)(2,1)S(1)}, u32[]{:S(2)}, u32[]{:S(2)}) collective-permute-start(bf16[144,896]{1,0:T(8,128)(2,1)S(1)} %add_convert_fusion.2), channel_id=1, source_target_pairs={{0,12},{4,8},{8,4},{12,0},{1,13},{5,9},{9,5},{13,1},{2,14},{6,10},... | collective-permute-start | bytes 774152 | tf_op jit(solution)/shard_map/ppermute | solution.py:35
  40.8 22.2 %collective-permute-start.8 = (bf16[144,896]{1,0:T(8,128)(2,1)S(1)}, bf16[144,896]{1,0:T(8,128)(2,1)S(1)}, u32[]{:S(2)}, u32[]{:S(2)}) collective-permute-start(bf16[144,896]{1,0:T(8,128)(2,1)S(1)} %add_convert_fusion.1), channel_id=1, source_target_pairs={{0,8},{4,12},{8,0},{12,4},{1,9},{5,13},{9,1},{13,5},{2,10},{6,14},... | collective-permute-start | bytes 774152 | tf_op jit(solution)/shard_map/ppermute | solution.py:35
  50.2 15.8 %collective-permute-start.10 = (bf16[144,896]{1,0:T(8,128)(2,1)S(1)}, bf16[144,896]{1,0:T(8,128)(2,1)S(1)}, u32[]{:S(2)}, u32[]{:S(2)}) collective-permute-start(bf16[144,896]{1,0:T(8,128)(2,1)S(1)} %add_convert_fusion), channel_id=1, source_target_pairs={{0,4},{4,0},{8,12},{12,8},{1,5},{5,1},{9,13},{13,9},{2,6},{6,2},{1... | collective-permute-start | bytes 774152 | tf_op jit(solution)/shard_map/ppermute | solution.py:35

commit v2 on v1

--- a/solution.py
+++ b/solution.py
@@ -13,6 +13,7 @@
 bf16, f32, i32 = jnp.bfloat16, jnp.float32, jnp.int32
 vmem = pl.BlockSpec(memory_space=pltpu.VMEM)
 smem = pl.BlockSpec(memory_space=pltpu.SMEM)
+hbm = pl.BlockSpec(memory_space=pltpu.HBM)
 
 
 def call(body, outs, in_specs, scratch=(), flops=0, moved=0, exps=0):
@@ -54,14 +55,23 @@
     return jnp.minimum(first_row, rows_dev - slot_rows)
 
 
-def pack_kernel(seq_size, frames_dev, slot_rows, partner, count_ref, grads_ref, *outs):
+def pack_kernel(seq_size, frames_dev, slot_rows, partner, count_hbm, grads_hbm, *refs):
+    *outs, count_ref, grads_ref, count_sem, grads_sem = refs
+    count_copy = pltpu.make_async_copy(count_hbm, count_ref, count_sem)
+    grads_copy = pltpu.make_async_copy(grads_hbm, grads_ref, grads_sem)
+    count_copy.start()
+    grads_copy.start()
+    count_copy.wait()
     my_seq = lax.axis_index("seq")
     rows_dev = grads_ref.shape[0]
     row = lax.broadcasted_iota(i32, (slot_rows, rows_dev), 0)
     column = lax.broadcasted_iota(i32, (slot_rows, rows_dev), 1)
+    starts = []
     for k in range(seq_size):
-        target = partner(my_seq, k)
-        start = slot_start(kept_before(count_ref, target * frames_dev), my_seq, seq_size, rows_dev, slot_rows)
+        begin = kept_before(count_ref, partner(my_seq, k) * frames_dev)
+        starts.append(slot_start(begin, my_seq, seq_size, rows_dev, slot_rows))
+    grads_copy.wait()
+    for k, start in enumerate(starts):
         picks = jnp.where(column == row + start, 1.0, 0.0).astype(bf16)
         rows = jnp.dot(picks, grads_ref[...], preferred_element_type=f32).astype(bf16)
         if len(outs) == 1:
@@ -115,26 +125,26 @@
     rows_t_ref[...] = rows_ref[...].T
 
 
-def grad_kernel(chunks, tile, slots_in, *refs):
+def grad_kernel(slots_in, chunks, tile, *refs):
     grads, (slope_ref, rows_t_ref, grad_ref), outs = refs[:slots_in], refs[slots_in:slots_in + 3], refs[slots_in + 3:]
     slot_rows = grads[0].shape[0]
     for k, ref in enumerate(grads):
         here = slice(k * slot_rows, (k + 1) * slot_rows)
         grad_ref[here, :] = (ref[...].astype(f32) * slope_ref[here, :]).astype(bf16)
-    weight_tiles(chunks, tile, rows_t_ref, grad_ref, outs)
-
-
-def weight_tiles(chunks, tile, rows_t_ref, grad_ref, outs):
+    weight_rows(chunks, tile, rows_t_ref, grad_ref, outs)
+
+
+def weight_rows(chunks, tile, rows_t_ref, grad_ref, outs):
     my_seq, my_dp = lax.axis_index("seq"), lax.axis_index("dp")
     videos = lax.axis_size("dp")
-    for (k, j), ref in zip(chunks, outs):
+    for (k, j, first, last), ref in zip(chunks, outs):
         owner = (my_seq ^ k) * videos + (my_dp ^ j)
-        rows = rows_t_ref[pl.ds(pl.multiple_of(owner * tile, 16), tile), :]
+        rows = rows_t_ref[pl.ds(pl.multiple_of(owner * tile + first, 16), last - first), :]
         ref[...] = jnp.dot(rows, grad_ref[...], preferred_element_type=f32).astype(ref.dtype)
 
 
-def tiles_kernel(chunks, tile, rows_t_ref, grad_ref, *outs):
-    weight_tiles(chunks, tile, rows_t_ref, grad_ref, outs)
+def rows_kernel(chunks, tile, rows_t_ref, grad_ref, *outs):
+    weight_rows(chunks, tile, rows_t_ref, grad_ref, outs)
 
 
 def row_kernel(grad_ref, weight_ref, own_ref, peer_ref):
@@ -142,11 +152,12 @@
     half = own_ref.shape[1]
     for ref, which in ((peer_ref, 1 - my_half), (own_ref, my_half)):
         part = weight_ref[pl.ds(pl.multiple_of(which * half, 16), half), :]
-        ref[...] = lax.dot_general(grad_ref[...], part, (((1,), (1,)), ((), ())), preferred_element_type=f32)
+        rows = lax.dot_general(grad_ref[...], part, (((1,), (1,)), ((), ())), preferred_element_type=f32)
+        ref[...] = rows.astype(ref.dtype)
 
 
 def place_kernel(own_ref, peer_ref, place_ref, out_ref):
-    rows = (own_ref[...] + peer_ref[...]).astype(bf16)
+    rows = (own_ref[...] + peer_ref[...].astype(f32)).astype(bf16)
     out_ref[...] = jnp.dot(place_ref[...], rows, preferred_element_type=f32).astype(bf16)
 
 
@@ -159,7 +170,7 @@
     slot_rows = (slot_rows + 15) // 16 * 16
     slots = seq_size * slot_rows
     tile = width // (seq_size * videos)
-    direct = seq_size <= 8 and videos <= 2 and tile % 16 == 0
+    direct = seq_size == 4 and videos == 2 and tile % 48 == 0
     norm_scale = 1.0 / math.sqrt(videos * seq_size * rows_dev)
 
     def partner(me, k):
@@ -171,7 +182,13 @@
     outgoing = call(
         functools.partial(pack_kernel, seq_size, frames_dev, slot_rows, partner),
         [one] * seq_size if direct else [shape(bf16, seq_size, slot_rows, hidden)],
-        [smem, vmem],
+        [hbm, hbm],
+        [
+            pltpu.SMEM(keep_count.shape, i32),
+            pltpu.VMEM((rows_dev, hidden), bf16),
+            pltpu.SemaphoreType.DMA(()),
+            pltpu.SemaphoreType.DMA(()),
+        ],
         flops=2 * slots * rows_dev * hidden,
         moved=2 * hidden * (rows_dev + slots),
     )(keep_count, local_grads)
@@ -190,37 +207,32 @@
         exps=2 * slots * hidden,
     )(keep_count, keep_order.reshape(frames_dev, patches), flat_tokens, weight, bias.reshape(1, hidden))
 
-    order = [k for k in range(seq_size - 1, -1, -1)]
-    sent = [(k, 1) for k in order] if direct and videos == 2 else []
-    own = [(k, 0) for k in order] if direct else []
-    tile_flops, tile_bytes = 2 * tile * slots * hidden, 4 * tile * hidden
-    slope_grad, *first = call(
-        functools.partial(grad_kernel, sent[:1], tile, len(arrived)),
-        [shape(bf16, slots, hidden)] + [shape(bf16, tile, hidden)] * len(sent[:1]),
-        [vmem] * (len(arrived) + 2),
-        flops=tile_flops,
-        moved=8 * slots * hidden + 2 * slots * width,
-    )(*arrived, slope, rows_t)
+    wide = shape(bf16, slots, hidden)
+    spans = [(3, 0, tile), (2, 0, tile), (1, 0, tile), (0, 0, tile)] if direct else []
+
+    def weight_part(body, chunks, dtypes, operands, extra=()):
+        rows = sum(last - first for _, _, first, last in chunks)
+        return call(
+            functools.partial(body, chunks, tile),
+            list(extra) + [shape(dtype, last - first, hidden) for dtype, (_, _, first, last) in zip(dtypes, chunks)],
+            [vmem] * len(operands),
+            flops=2 * rows * slots * hidden,
+            moved=4 * rows * hidden + 2 * slots * (rows + hidden),
+        )(*operands)
+
+    sent = [(k, 1, first, last) for k, first, last in spans]
+    own = [(k, 0, first, last) for k, first, last in spans]
+    slope_grad, *to_dp = weight_part(
+        functools.partial(grad_kernel, len(arrived)), sent[:1], [bf16], [*arrived, slope, rows_t], [wide]
+    )
     if direct:
-        rest = call(
-            functools.partial(tiles_kernel, sent[1:], tile),
-            [shape(bf16, tile, hidden)] * len(sent[1:]),
-            [vmem, vmem],
-            flops=tile_flops * len(sent[1:]),
-            moved=tile_bytes * len(sent[1:]),
-        )(rows_t, slope_grad) if sent[1:] else []
-        mine = call(
-            functools.partial(tiles_kernel, own, tile),
-            [shape(f32, tile, hidden)] * len(own),
-            [vmem, vmem],
-            flops=tile_flops * len(own),
-            moved=tile_bytes * len(own),
-        )(rows_t, slope_grad)
-        from_dp = [exchanged(part, "dp", 1) for part in first + list(rest)]
-        sums = [part + peer.astype(f32) for part, peer in zip(mine, from_dp)] if sent else mine
-        summed = sums[-1]
-        for k, part in zip(order[:-1], sums[:-1]):
-            summed = summed + exchanged(part.astype(bf16), "seq", k).astype(f32)
+        to_dp += weight_part(rows_kernel, sent[1:], [bf16] * 3, [rows_t, slope_grad])
+        far, second, near, home = weight_part(rows_kernel, own, [f32] * 4, [rows_t, slope_grad])
+        got, home_out = lax.optimization_barrier((exchanged(to_dp[0], "dp", 1), to_dp[3]))
+        far = exchanged((far + got.astype(f32)).astype(bf16), "seq", 3)
+        second = exchanged((second + exchanged(to_dp[1], "dp", 1).astype(f32)).astype(bf16), "seq", 2)
+        near = exchanged((near + exchanged(to_dp[2], "dp", 1).astype(f32)).astype(bf16), "seq", 1)
+        home = home + exchanged(home_out, "dp", 1).astype(f32)
     else:
         partial = jnp.dot(rows_t, slope_grad, preferred_element_type=f32)
         summed = lax.psum_scatter(partial, ("seq", "dp"), scatter_dimension=0, tiled=True)
@@ -228,7 +240,7 @@
     half = width // lax.axis_size("mp")
     own_part, peer_part = call(
         row_kernel,
-        [shape(f32, slots, half)] * 2,
+        [shape(f32, slots, half), shape(bf16, slots, half)],
         [vmem, vmem],
         flops=2 * slots * width * hidden,
         moved=2 * hidden * (slots + width) + 4 * slots * width,
@@ -241,6 +253,9 @@
         flops=2 * tokens * slots * half,
         moved=2 * tokens * (slots + half) + 8 * slots * half,
     )(own_part, peer_part, place)
+    if direct:
+        home, grid = lax.optimization_barrier((home, grid))
+        summed = home + far.astype(f32) + second.astype(f32) + near.astype(f32)
     return (grid.reshape(1, frames_dev, patches, half), summed * norm_scale)
 
 

time: 69 us -> 64.4 us (0.933)
  starting transfers between devices: 26.4 us -> 23.6 us
  waiting for transfers between devices: 22.1 us -> 20.2 us
    ppermute x11, starting transfers between devices: 26.4 us -> 23.6 us  [exchanged(): lax.ppermute(array, axis, [(i, i ^ distance) for i in range(lax.axis_size...]
    ppermute x11, waiting for transfers between devices: 22.1 us -> 20.2 us  [exchanged(): lax.ppermute(array, axis, [(i, i ^ distance) for i in range(lax.axis_size...]
  transfers between devices with their start and end apart: 11 -> 11, of which waited for: 5 -> 4; matrix products, arithmetic and copies ran while one was open for 3% -> 1% of each run, Pallas kernels for 13% -> 17%
where the time goes in v2:
time: 64.4 us; the launch traced here: 64.1 us
  starting transfers between devices  23.6 us (37%)
  waiting for transfers between devices  20.2 us (31%)
  Pallas kernels  12.5 us (19%)
  local copies, waits for them, and re-layouts  5.95 us (9%)
  other arithmetic  1.15 us (2%)
  between operations  0.73 us (1%)
    ppermute x11, starting transfers between devices, exchanged(): lax.ppermute(array, axis, [(i, i ^ distance) for i in range(lax.axis_size...  23.6 us
    ppermute x11, waiting for transfers between devices, exchanged(): lax.ppermute(array, axis, [(i, i ^ distance) for i in range(lax.axis_size...  20.2 us
    unnamed x12, local copies, waits for them, and re-layouts  5.26 us
    pallas_call x1, Pallas kernels, shards(): call(functools.partial(slope_kernel, seq_size, rows_dev, slot_rows, partn...  5.23 us
    pallas_call x3, Pallas kernels, weight_part(): call(functools.partial(body, chunks, tile), list(extra) + [shape(dtype, l...  2.48 us
    pallas_call x1, Pallas kernels, shards(): call(row_kernel, [shape(f32, slots, half), shape(bf16, slots, half)], [vm...  1.96 us
    pallas_call x1, Pallas kernels, shards(): call(place_kernel, [shape(bf16, tokens, half)], [vmem] * 3, flops=2 * tok...  1.69 us
  transfers between devices with their start and end apart: 11, of which 4 were waited for; matrix products, arithmetic and copies ran while one was open for 1% of the time, Pallas kernels for 17%

profile of v2, /device:TPU:0, one launch (start us, length us, event | category | flops | bytes accessed | tf_op | source)
XLA Modules:
  0.0 64.1 jit_solution(12932991765520789369)
XLA Ops:
  0.6 0.0 copy-start.3
  0.6 1.0 %copy-done.3 = bf16[1,256,1,896]{3,1,2,0:T(8,128)(2,1)S(1)} copy-done((bf16[1,256,1,896]{3,1,2,0:T(8,128)(2,1)S(1)}, bf16[1,256,1,896]{3,1,2,0:T(8,128)(2,1)}, u32[]{:S(2)}) %copy-start.3) | copy-done | bytes 458776
  1.6 0.0 copy-start.5
  1.7 0.7 %copy-done.5 = s32[1,16]{1,0:T(1,128)S(1)} copy-done((s32[1,16]{1,0:T(1,128)S(1)}, s32[1,16]{1,0:T(1,128)}, u32[]{:S(2)}) %copy-start.5) | copy-done | bytes 88
  2.3 1.1 %shard_map.78 = (bf16[144,896]{1,0:T(8,128)(2,1)S(1)}, bf16[144,896]{1,0:T(8,128)(2,1)S(1)}, bf16[144,896]{1,0:T(8,128)(2,1)S(1)}, bf16[144,896]{1,0:T(8,128)(2,1)S(1)}) custom-call(s32[1,16]{1,0:T(1,128)S(1)} %copy-done.5, bf16[256,896]{1,0:T(8,128)(2,1)S(1)} %bitcast.5), custom_call_target="tpu_custom_call" | custom-call | flops 264241152 | bytes 1490944 | tf_op jit(solution)/shard_map/pallas_call | solution.py:182
  3.4 3.1 %collective-permute-start = (bf16[144,896]{1,0:T(8,128)(2,1)S(1)}, bf16[144,896]{1,0:T(8,128)(2,1)S(1)}, u32[]{:S(2)}, u32[]{:S(2)}) collective-permute-start(bf16[144,896]{1,0:T(8,128)(2,1)S(1)} %get-tuple-element.26), channel_id=1, source_target_pairs={{0,4},{4,0},{8,12},{12,8},{1,5},{5,1},{9,13},{13,9},{2,6},{6,2},{1... | collective-permute-start | bytes 774152 | tf_op jit(solution)/shard_map/ppermute | solution.py:36
  6.5 2.6 %collective-permute-start.1 = (bf16[144,896]{1,0:T(8,128)(2,1)S(1)}, bf16[144,896]{1,0:T(8,128)(2,1)S(1)}, u32[]{:S(2)}, u32[]{:S(2)}) collective-permute-start(bf16[144,896]{1,0:T(8,128)(2,1)S(1)} %get-tuple-element.27), channel_id=1, source_target_pairs={{0,8},{4,12},{8,0},{12,4},{1,9},{5,13},{9,1},{13,5},{2,10},{6,14},... | collective-permute-start | bytes 774152 | tf_op jit(solution)/shard_map/ppermute | solution.py:36
  9.1 0.0 collective-permute-start.2
  9.1 0.7 %reshape.21.bias_ref = f32[1,896]{1,0:T(1,128)S(1)} reshape(f32[896]{0:T(1024)} %param.9) | data formatting | bytes 7168 | tf_op jit(solution)/shard_map/reshape | solution.py:208
  9.8 0.0 copy-start
  9.8 1.6 %copy-done = bf16[1152,896]{1,0:T(8,128)(2,1)S(1)} copy-done((bf16[1152,896]{1,0:T(8,128)(2,1)S(1)}, bf16[1152,896]{1,0:T(8,128)(2,1)}, u32[]{:S(2)}) %copy-start) | copy-done | bytes 2064408
  11.4 0.0 copy-start.2
  11.4 1.3 %copy-done.2 = bf16[1,4,144,1152]{3,2,1,0:T(8,128)(2,1)S(1)} copy-done((bf16[1,4,144,1152]{3,2,1,0:T(8,128)(2,1)S(1)}, bf16[1,4,144,1152]{3,2,1,0:T(8,128)(2,1)}, u32[]{:S(2)}) %copy-start.2) | copy-done | bytes 1327128
  12.7 0.0 copy-start.4
  12.7 0.7 %copy-done.4 = s32[1,4,144]{2,1,0:T(4,128)S(1)} copy-done((s32[1,4,144]{2,1,0:T(4,128)S(1)}, s32[1,4,144]{2,1,0:T(4,128)}, u32[]{:S(2)}) %copy-start.4) | copy-done | bytes 2328
  13.4 5.2 %shard_map.77 = (f32[576,896]{1,0:T(8,128)S(1)}, bf16[1152,576]{1,0:T(8,128)(2,1)S(1)}, bf16[576,576]{1,0:T(8,128)(2,1)S(1)}) custom-call(s32[1,16]{1,0:T(1,128)S(1)} %copy-done.5, s32[4,144]{1,0:T(4,128)S(1)} %bitcast.6, bf16[576,1152]{1,0:T(8,128)(2,1)S(1)} %bitcast.4, bf16[1152,896]{1,0:T(8,128)(2,1)S(1)} %copy-done, f32[1,896]{1,0:T(1,128)S(1)} %reshape.21.bias_ref), custom_call_target="tpu_custom_call" | custom-call | flops 1953497088 | bytes 6782976 | tf_op jit(solution)/shard_map/pallas_call | solution.py:200
  18.6 0.0 collective-permute-done.refs_1_
  18.6 9.0 %collective-permute-done.1.refs_2_ = bf16[144,896]{1,0:T(8,128)(2,1)S(1)} collective-permute-done((bf16[144,896]{1,0:T(8,128)(2,1)S(1)}, bf16[144,896]{1,0:T(8,128)(2,1)S(1)}, u32[]{:S(2)}, u32[]{:S(2)}) %collective-permute-start.1) | collective-permute-done | bytes 258080 | tf_op jit(solution)/shard_map/ppermute | solution.py:36
  27.6 0.0 collective-permute-done.2.refs_3_
  27.6 0.5 shard_map.79
  28.1 0.0 copy-start.1
  28.2 1.6 %collective-permute-start.3 = (bf16[144,896]{1,0:T(8,128)(2,1)S(1)}, bf16[144,896]{1,0:T(8,128)(2,1)S(1)}, u32[]{:S(2)}, u32[]{:S(2)}) collective-permute-start(bf16[144,896]{1,0:T(8,128)(2,1)S(1)} %get-tuple-element.32), channel_id=1, source_target_pairs={{0,2},{2,0},{1,3},{3,1},{4,6},{6,4},{5,7},{7,5},{8,10},{10,8},{9,1... | collective-permute-start | bytes 774152 | tf_op jit(solution)/shard_map/ppermute | solution.py:36
  29.7 0.9 %shard_map.81 = (bf16[144,896]{1,0:T(8,128)(2,1)S(1)}, bf16[144,896]{1,0:T(8,128)(2,1)S(1)}, bf16[144,896]{1,0:T(8,128)(2,1)S(1)}) custom-call(bf16[1152,576]{1,0:T(8,128)(2,1)S(1)} %get-tuple-element.24.refs_5_.rows_t_ref, bf16[576,896]{1,0:T(8,128)(2,1)S(1)} %get-tuple-element.30.grad_ref), custom_call_target="tpu_custom_call" | custom-call | flops 445906944 | bytes 3078144 | tf_op jit(solution)/shard_map/pallas_call | solution.py:215
  30.6 0.6 collective-permute-start.7
  31.2 0.0 copy-done.1
  31.2 2.0 %shard_map.82 = (f32[576,576]{1,0:T(8,128)S(1)}, bf16[576,576]{1,0:T(8,128)(2,1)S(1)}) custom-call(bf16[576,896]{1,0:T(8,128)(2,1)S(1)} %get-tuple-element.30.grad_ref, bf16[1152,896]{1,0:T(8,128)(2,1)S(1)} %copy-done.1), custom_call_target="tpu_custom_call" | custom-call | flops 1189085184 | bytes 5750784 | tf_op jit(solution)/shard_map/pallas_call | solution.py:241
  33.2 1.1 %shard_map.80 = (f32[144,896]{1,0:T(8,128)S(1)}, f32[144,896]{1,0:T(8,128)S(1)}, f32[144,896]{1,0:T(8,128)S(1)}, f32[144,896]{1,0:T(8,128)S(1)}) custom-call(bf16[1152,576]{1,0:T(8,128)(2,1)S(1)} %get-tuple-element.24.refs_5_.rows_t_ref, bf16[576,896]{1,0:T(8,128)(2,1)S(1)} %get-tuple-element.30.grad_ref), custom_call_target="tpu_custom_call" | custom-call | flops 594542592 | bytes 3760128 | tf_op jit(solution)/shard_map/pallas_call | solution.py:215
  34.3 1.6 %collective-permute-start.9 = (bf16[144,896]{1,0:T(8,128)(2,1)S(1)}, bf16[144,896]{1,0:T(8,128)(2,1)S(1)}, u32[]{:S(2)}, u32[]{:S(2)}) collective-permute-start(bf16[144,896]{1,0:T(8,128)(2,1)S(1)} %get-tuple-element.45), channel_id=1, source_target_pairs={{0,2},{2,0},{1,3},{3,1},{4,6},{6,4},{5,7},{7,5},{8,10},{10,8},{9,1... | collective-permute-start | bytes 774152 | tf_op jit(solution)/shard_map/ppermute | solution.py:36
  35.8 0.0 collective-permute-start.5
  35.9 1.5 %collective-permute-done.3 = bf16[144,896]{1,0:T(8,128)(2,1)S(1)} collective-permute-done((bf16[144,896]{1,0:T(8,128)(2,1)S(1)}, bf16[144,896]{1,0:T(8,128)(2,1)S(1)}, u32[]{:S(2)}, u32[]{:S(2)}) %collective-permute-start.3) | collective-permute-done | bytes 258080 | tf_op jit(solution)/shard_map/ppermute | solution.py:36
  37.4 1.5 %collective-permute-start.4 = (bf16[144,896]{1,0:T(8,128)(2,1)S(1)}, bf16[144,896]{1,0:T(8,128)(2,1)S(1)}, u32[]{:S(2)}, u32[]{:S(2)}) collective-permute-start(bf16[144,896]{1,0:T(8,128)(2,1)S(1)} %get-tuple-element.34), channel_id=1, source_target_pairs={{0,2},{2,0},{1,3},{3,1},{4,6},{6,4},{5,7},{7,5},{8,10},{10,8},{9,1... | collective-permute-start | bytes 774152 | tf_op jit(solution)/shard_map/ppermute | solution.py:36
  38.9 0.1 add_convert_fusion.2
  38.9 2.5 %collective-permute-start.6 = (bf16[144,896]{1,0:T(8,128)(2,1)S(1)}, bf16[144,896]{1,0:T(8,128)(2,1)S(1)}, u32[]{:S(2)}, u32[]{:S(2)}) collective-permute-start(bf16[144,896]{1,0:T(8,128)(2,1)S(1)} %add_convert_fusion.2), channel_id=1, source_target_pairs={{0,12},{4,8},{8,4},{12,0},{1,13},{5,9},{9,5},{13,1},{2,14},{6,10},... | collective-permute-start | bytes 774152 | tf_op jit(solution)/shard_map/ppermute | solution.py:36
  41.5 1.5 %collective-permute-done.7 = bf16[144,896]{1,0:T(8,128)(2,1)S(1)} collective-permute-done((bf16[144,896]{1,0:T(8,128)(2,1)S(1)}, bf16[144,896]{1,0:T(8,128)(2,1)S(1)}, u32[]{:S(2)}, u32[]{:S(2)}) %collective-permute-start.7) | collective-permute-done | bytes 258080 | tf_op jit(solution)/shard_map/ppermute | solution.py:36
  42.9 0.1 add_convert_fusion.1
  43.0 5.7 %collective-permute-start.8 = (bf16[144,896]{1,0:T(8,128)(2,1)S(1)}, bf16[144,896]{1,0:T(8,128)(2,1)S(1)}, u32[]{:S(2)}, u32[]{:S(2)}) collective-permute-start(bf16[144,896]{1,0:T(8,128)(2,1)S(1)} %add_convert_fusion.1), channel_id=1, source_target_pairs={{0,8},{4,12},{8,0},{12,4},{1,9},{5,13},{9,1},{13,5},{2,10},{6,14},... | collective-permute-start | bytes 774152 | tf_op jit(solution)/shard_map/ppermute | solution.py:36
  48.7 0.0 collective-permute-done.9
  48.7 0.1 add_convert_fusion
  48.8 4.4 %collective-permute-start.10 = (bf16[144,896]{1,0:T(8,128)(2,1)S(1)}, bf16[144,896]{1,0:T(8,128)(2,1)S(1)}, u32[]{:S(2)}, u32[]{:S(2)}) collective-permute-start(bf16[144,896]{1,0:T(8,128)(2,1)S(1)} %add_convert_fusion), channel_id=1, source_target_pairs={{0,4},{4,0},{8,12},{12,8},{1,5},{5,1},{9,13},{13,9},{2,6},{6,2},{1... | collective-permute-start | bytes 774152 | tf_op jit(solution)/shard_map/ppermute | solution.py:36
  53.2 0.0 collective-permute-done.4
  53.3 0.0 collective-permute-done.5.peer_ref
  53.3 1.7 %shard_map.83 = bf16[576,576]{1,0:T(8,128)(2,1)} custom-call(f32[576,576]{1,0:T(8,128)S(1)} %get-tuple-element.35.own_ref, bf16[576,576]{1,0:T(8,128)(2,1)S(1)} %collective-permute-done.5.peer_ref, bf16[576,576]{1,0:T(8,128)(2,1)S(1)} %get-tuple-element.37.place_ref), custom_call_target="tpu_custom_call" | custom-call | flops 382205952 | bytes 3981312 | tf_op jit(solution)/shard_map/pallas_call | solution.py:249
  55.0 0.0 collective-permute-done.6
  55.0 8.2 %collective-permute-done.8 = bf16[144,896]{1,0:T(8,128)(2,1)S(1)} collective-permute-done((bf16[144,896]{1,0:T(8,128)(2,1)S(1)}, bf16[144,896]{1,0:T(8,128)(2,1)S(1)}, u32[]{:S(2)}, u32[]{:S(2)}) %collective-permute-start.8) | collective-permute-done | bytes 258080 | tf_op jit(solution)/shard_map/ppermute | solution.py:36
  63.2 0.0 collective-permute-done.10
  63.2 0.9 %add_multiply_fusion = f32[144,896]{1,0:T(8,128)} fusion(bf16[144,896]{1,0:T(8,128)(2,1)S(1)} %collective-permute-done.10, bf16[144,896]{1,0:T(8,128)(2,1)S(1)} %collective-permute-done.8, f32[144,896]{1,0:T(8,128)S(1)} %convert_add_fusion, bf16[144,896]{1,0:T(8,128)(2,1)S(1)} %collective-permute-done.6), kind=kLoop, calls=%fused_computation | loop fusion | flops 903168 | bytes 1806336 | tf_op jit(solution)/shard_map/mul | solution.py:259
  (1 shorter events, 0.0 us)
Async XLA Ops:
  0.6 1.0 %copy-start.3 = (bf16[1,256,1,896]{3,1,2,0:T(8,128)(2,1)S(1)}, bf16[1,256,1,896]{3,1,2,0:T(8,128)(2,1)}, u32[]{:S(2)}) copy-start(bf16[1,256,1,896]{3,1,2,0:T(8,128)(2,1)} %param.7) | copy-start | bytes 1376260
  1.6 0.7 %copy-start.5 = (s32[1,16]{1,0:T(1,128)S(1)}, s32[1,16]{1,0:T(1,128)}, u32[]{:S(2)}) copy-start(s32[1,16]{1,0:T(1,128)} %count_hbm.1) | copy-start | bytes 196
  3.4 15.2 %collective-permute-start = (bf16[144,896]{1,0:T(8,128)(2,1)S(1)}, bf16[144,896]{1,0:T(8,128)(2,1)S(1)}, u32[]{:S(2)}, u32[]{:S(2)}) collective-permute-start(bf16[144,896]{1,0:T(8,128)(2,1)S(1)} %get-tuple-element.26), channel_id=1, source_target_pairs={{0,4},{4,0},{8,12},{12,8},{1,5},{5,1},{9,13},{13,9},{2,6},{6,2},{1... | collective-permute-start | bytes 774152 | tf_op jit(solution)/shard_map/ppermute | solution.py:36
  6.5 21.1 %collective-permute-start.1 = (bf16[144,896]{1,0:T(8,128)(2,1)S(1)}, bf16[144,896]{1,0:T(8,128)(2,1)S(1)}, u32[]{:S(2)}, u32[]{:S(2)}) collective-permute-start(bf16[144,896]{1,0:T(8,128)(2,1)S(1)} %get-tuple-element.27), channel_id=1, source_target_pairs={{0,8},{4,12},{8,0},{12,4},{1,9},{5,13},{9,1},{13,5},{2,10},{6,14},... | collective-permute-start | bytes 774152 | tf_op jit(solution)/shard_map/ppermute | solution.py:36
  9.1 18.5 %collective-permute-start.2 = (bf16[144,896]{1,0:T(8,128)(2,1)S(1)}, bf16[144,896]{1,0:T(8,128)(2,1)S(1)}, u32[]{:S(2)}, u32[]{:S(2)}) collective-permute-start(bf16[144,896]{1,0:T(8,128)(2,1)S(1)} %get-tuple-element.28), channel_id=1, source_target_pairs={{0,12},{4,8},{8,4},{12,0},{1,13},{5,9},{9,5},{13,1},{2,14},{6,10},... | collective-permute-start | bytes 774152 | tf_op jit(solution)/shard_map/ppermute | solution.py:36
  9.8 1.6 %copy-start = (bf16[1152,896]{1,0:T(8,128)(2,1)S(1)}, bf16[1152,896]{1,0:T(8,128)(2,1)}, u32[]{:S(2)}) copy-start(bf16[1152,896]{1,0:T(8,128)(2,1)} %weight_ref.3) | copy-start | bytes 6193156
  11.4 1.3 %copy-start.2 = (bf16[1,4,144,1152]{3,2,1,0:T(8,128)(2,1)S(1)}, bf16[1,4,144,1152]{3,2,1,0:T(8,128)(2,1)}, u32[]{:S(2)}) copy-start(bf16[1,4,144,1152]{3,2,1,0:T(8,128)(2,1)} %param.6) | copy-start | bytes 3981316
  12.7 0.7 %copy-start.4 = (s32[1,4,144]{2,1,0:T(4,128)S(1)}, s32[1,4,144]{2,1,0:T(4,128)}, u32[]{:S(2)}) copy-start(s32[1,4,144]{2,1,0:T(4,128)} %param.11) | copy-start | bytes 6916
  28.1 3.0 %copy-start.1 = (bf16[1152,896]{1,0:T(8,128)(2,1)S(1)}, bf16[1152,896]{1,0:T(8,128)(2,1)}, u32[]{:S(2)}) copy-start(bf16[1152,896]{1,0:T(8,128)(2,1)} %weight_ref.3) | copy-start | bytes 6193156
  28.2 9.2 %collective-permute-start.3 = (bf16[144,896]{1,0:T(8,128)(2,1)S(1)}, bf16[144,896]{1,0:T(8,128)(2,1)S(1)}, u32[]{:S(2)}, u32[]{:S(2)}) collective-permute-start(bf16[144,896]{1,0:T(8,128)(2,1)S(1)} %get-tuple-element.32), channel_id=1, source_target_pairs={{0,2},{2,0},{1,3},{3,1},{4,6},{6,4},{5,7},{7,5},{8,10},{10,8},{9,1... | collective-permute-start | bytes 774152 | tf_op jit(solution)/shard_map/ppermute | solution.py:36
  30.6 12.3 %collective-permute-start.7 = (bf16[144,896]{1,0:T(8,128)(2,1)S(1)}, bf16[144,896]{1,0:T(8,128)(2,1)S(1)}, u32[]{:S(2)}, u32[]{:S(2)}) collective-permute-start(bf16[144,896]{1,0:T(8,128)(2,1)S(1)} %get-tuple-element.43), channel_id=1, source_target_pairs={{0,2},{2,0},{1,3},{3,1},{4,6},{6,4},{5,7},{7,5},{8,10},{10,8},{9,1... | collective-permute-start | bytes 774152 | tf_op jit(solution)/shard_map/ppermute | solution.py:36
  34.3 14.5 %collective-permute-start.9 = (bf16[144,896]{1,0:T(8,128)(2,1)S(1)}, bf16[144,896]{1,0:T(8,128)(2,1)S(1)}, u32[]{:S(2)}, u32[]{:S(2)}) collective-permute-start(bf16[144,896]{1,0:T(8,128)(2,1)S(1)} %get-tuple-element.45), channel_id=1, source_target_pairs={{0,2},{2,0},{1,3},{3,1},{4,6},{6,4},{5,7},{7,5},{8,10},{10,8},{9,1... | collective-permute-start | bytes 774152 | tf_op jit(solution)/shard_map/ppermute | solution.py:36
  35.8 17.4 %collective-permute-start.5 = (bf16[576,576]{1,0:T(8,128)(2,1)S(1)}, bf16[576,576]{1,0:T(8,128)(2,1)S(1)}, u32[]{:S(2)}, u32[]{:S(2)}) collective-permute-start(bf16[576,576]{1,0:T(8,128)(2,1)S(1)} %get-tuple-element.36), channel_id=1, source_target_pairs={{0,1},{1,0},{2,3},{3,2},{4,5},{5,4},{6,7},{7,6},{8,9},{9,8},{10,11... | collective-permute-start | bytes 1990664 | tf_op jit(solution)/shard_map/ppermute | solution.py:36
  37.4 15.8 %collective-permute-start.4 = (bf16[144,896]{1,0:T(8,128)(2,1)S(1)}, bf16[144,896]{1,0:T(8,128)(2,1)S(1)}, u32[]{:S(2)}, u32[]{:S(2)}) collective-permute-start(bf16[144,896]{1,0:T(8,128)(2,1)S(1)} %get-tuple-element.34), channel_id=1, source_target_pairs={{0,2},{2,0},{1,3},{3,1},{4,6},{6,4},{5,7},{7,5},{8,10},{10,8},{9,1... | collective-permute-start | bytes 774152 | tf_op jit(solution)/shard_map/ppermute | solution.py:36
  38.9 16.0 %collective-permute-start.6 = (bf16[144,896]{1,0:T(8,128)(2,1)S(1)}, bf16[144,896]{1,0:T(8,128)(2,1)S(1)}, u32[]{:S(2)}, u32[]{:S(2)}) collective-permute-start(bf16[144,896]{1,0:T(8,128)(2,1)S(1)} %add_convert_fusion.2), channel_id=1, source_target_pairs={{0,12},{4,8},{8,4},{12,0},{1,13},{5,9},{9,5},{13,1},{2,14},{6,10},... | collective-permute-start | bytes 774152 | tf_op jit(solution)/shard_map/ppermute | solution.py:36
  43.0 20.2 %collective-permute-start.8 = (bf16[144,896]{1,0:T(8,128)(2,1)S(1)}, bf16[144,896]{1,0:T(8,128)(2,1)S(1)}, u32[]{:S(2)}, u32[]{:S(2)}) collective-permute-start(bf16[144,896]{1,0:T(8,128)(2,1)S(1)} %add_convert_fusion.1), channel_id=1, source_target_pairs={{0,8},{4,12},{8,0},{12,4},{1,9},{5,13},{9,1},{13,5},{2,10},{6,14},... | collective-permute-start | bytes 774152 | tf_op jit(solution)/shard_map/ppermute | solution.py:36
  48.8 14.4 %collective-permute-start.10 = (bf16[144,896]{1,0:T(8,128)(2,1)S(1)}, bf16[144,896]{1,0:T(8,128)(2,1)S(1)}, u32[]{:S(2)}, u32[]{:S(2)}) collective-permute-start(bf16[144,896]{1,0:T(8,128)(2,1)S(1)} %add_convert_fusion), channel_id=1, source_target_pairs={{0,4},{4,0},{8,12},{12,8},{1,5},{5,1},{9,13},{13,9},{2,6},{6,2},{1... | collective-permute-start | bytes 774152 | tf_op jit(solution)/shard_map/ppermute | solution.py:36

commit v3 on v2

--- a/solution.py
+++ b/solution.py
@@ -16,14 +16,14 @@
 hbm = pl.BlockSpec(memory_space=pltpu.HBM)
 
 
-def call(body, outs, in_specs, scratch=(), flops=0, moved=0, exps=0):
+def call(body, outs, in_specs, scratch=(), flops=0, moved=0, exps=0, vmem_mib=40):
     return pl.pallas_call(
         body,
         out_shape=outs,
         in_specs=in_specs,
         out_specs=[vmem] * len(outs),
         scratch_shapes=list(scratch),
-        compiler_params=pltpu.CompilerParams(vmem_limit_bytes=40 << 20),
+        compiler_params=pltpu.CompilerParams(vmem_limit_bytes=vmem_mib << 20),
         cost_estimate=pl.CostEstimate(flops=flops, bytes_accessed=moved, transcendentals=exps),
     )
 
@@ -137,17 +137,14 @@
 def weight_rows(chunks, tile, rows_t_ref, grad_ref, outs):
     my_seq, my_dp = lax.axis_index("seq"), lax.axis_index("dp")
     videos = lax.axis_size("dp")
-    for (k, j, first, last), ref in zip(chunks, outs):
+    for (k, j), ref in zip(chunks, outs):
         owner = (my_seq ^ k) * videos + (my_dp ^ j)
-        rows = rows_t_ref[pl.ds(pl.multiple_of(owner * tile + first, 16), last - first), :]
+        rows = rows_t_ref[pl.ds(pl.multiple_of(owner * tile, 16), tile), :]
         ref[...] = jnp.dot(rows, grad_ref[...], preferred_element_type=f32).astype(ref.dtype)
 
 
-def rows_kernel(chunks, tile, rows_t_ref, grad_ref, *outs):
+def rest_kernel(chunks, tile, rows_t_ref, grad_ref, weight_ref, own_ref, peer_ref, *outs):
     weight_rows(chunks, tile, rows_t_ref, grad_ref, outs)
-
-
-def row_kernel(grad_ref, weight_ref, own_ref, peer_ref):
     my_half = lax.axis_index("mp")
     half = own_ref.shape[1]
     for ref, which in ((peer_ref, 1 - my_half), (own_ref, my_half)):
@@ -170,7 +167,7 @@
     slot_rows = (slot_rows + 15) // 16 * 16
     slots = seq_size * slot_rows
     tile = width // (seq_size * videos)
-    direct = seq_size == 4 and videos == 2 and tile % 48 == 0
+    direct = seq_size == 4 and videos == 2 and tile % 16 == 0
     norm_scale = 1.0 / math.sqrt(videos * seq_size * rows_dev)
 
     def partner(me, k):
@@ -189,11 +186,13 @@
             pltpu.SemaphoreType.DMA(()),
             pltpu.SemaphoreType.DMA(()),
         ],
+        vmem_mib=60,
         flops=2 * slots * rows_dev * hidden,
         moved=2 * hidden * (rows_dev + slots),
     )(keep_count, local_grads)
     if direct:
-        arrived = [exchanged(rows, "seq", k) if k else rows for k, rows in enumerate(outgoing)]
+        arrived = [exchanged(outgoing[k], "seq", k) for k in range(seq_size - 1, 0, -1)] + [outgoing[0]]
+        arrived = arrived[::-1]
     else:
         arrived = [lax.all_to_all(outgoing[0], "seq", split_axis=0, concat_axis=0, tiled=True).reshape(slots, hidden)]
 
@@ -207,44 +206,30 @@
         exps=2 * slots * hidden,
     )(keep_count, keep_order.reshape(frames_dev, patches), flat_tokens, weight, bias.reshape(1, hidden))
 
-    wide = shape(bf16, slots, hidden)
-    spans = [(3, 0, tile), (2, 0, tile), (1, 0, tile), (0, 0, tile)] if direct else []
-
-    def weight_part(body, chunks, dtypes, operands, extra=()):
-        rows = sum(last - first for _, _, first, last in chunks)
-        return call(
-            functools.partial(body, chunks, tile),
-            list(extra) + [shape(dtype, last - first, hidden) for dtype, (_, _, first, last) in zip(dtypes, chunks)],
-            [vmem] * len(operands),
-            flops=2 * rows * slots * hidden,
-            moved=4 * rows * hidden + 2 * slots * (rows + hidden),
-        )(*operands)
-
-    sent = [(k, 1, first, last) for k, first, last in spans]
-    own = [(k, 0, first, last) for k, first, last in spans]
-    slope_grad, *to_dp = weight_part(
-        functools.partial(grad_kernel, len(arrived)), sent[:1], [bf16], [*arrived, slope, rows_t], [wide]
-    )
-    if direct:
-        to_dp += weight_part(rows_kernel, sent[1:], [bf16] * 3, [rows_t, slope_grad])
-        far, second, near, home = weight_part(rows_kernel, own, [f32] * 4, [rows_t, slope_grad])
-        got, home_out = lax.optimization_barrier((exchanged(to_dp[0], "dp", 1), to_dp[3]))
-        far = exchanged((far + got.astype(f32)).astype(bf16), "seq", 3)
-        second = exchanged((second + exchanged(to_dp[1], "dp", 1).astype(f32)).astype(bf16), "seq", 2)
-        near = exchanged((near + exchanged(to_dp[2], "dp", 1).astype(f32)).astype(bf16), "seq", 1)
-        home = home + exchanged(home_out, "dp", 1).astype(f32)
-    else:
-        partial = jnp.dot(rows_t, slope_grad, preferred_element_type=f32)
-        summed = lax.psum_scatter(partial, ("seq", "dp"), scatter_dimension=0, tiled=True)
-
     half = width // lax.axis_size("mp")
-    own_part, peer_part = call(
-        row_kernel,
-        [shape(f32, slots, half), shape(bf16, slots, half)],
-        [vmem, vmem],
-        flops=2 * slots * width * hidden,
-        moved=2 * hidden * (slots + width) + 4 * slots * width,
-    )(slope_grad, weight)
+    early, late = ((3, 2), (1, 0)) if direct else ((), ())
+
+    def both(tiles):
+        chunks = [(k, j) for j in (1, 0) for k in tiles]
+        outs = [shape(bf16 if j else f32, tile, hidden) for _, j in chunks]
+        return chunks, outs, 2 * sum(out.size for out in outs) * slots
+
+    chunks, outs, flops = both(early)
+    slope_grad, *first = call(
+        functools.partial(grad_kernel, len(arrived), chunks, tile),
+        [shape(bf16, slots, hidden), *outs],
+        [vmem] * (len(arrived) + 2),
+        flops=flops,
+        moved=8 * slots * hidden + 2 * slots * width,
+    )(*arrived, slope, rows_t)
+    chunks, outs, flops = both(late)
+    own_part, peer_part, *rest = call(
+        functools.partial(rest_kernel, chunks, tile),
+        [shape(f32, slots, half), shape(bf16, slots, half), *outs],
+        [vmem] * 3,
+        flops=flops + 2 * slots * width * hidden,
+        moved=2 * hidden * (slots + width) + 3 * slots * width,
+    )(rows_t, slope_grad, weight)
     peer_part = exchanged(peer_part, "mp", 1)
     (grid,) = call(
         place_kernel,
@@ -254,8 +239,19 @@
         moved=2 * tokens * (slots + half) + 8 * slots * half,
     )(own_part, peer_part, place)
     if direct:
+        far_out, second_out, far, second = first
+        near_out, home_out, near, home = rest
+        got, near_out = lax.optimization_barrier((exchanged(far_out, "dp", 1), near_out))
+        relayed = exchanged((far + got.astype(f32)).astype(bf16), "seq", 1).astype(f32)
+        got, home_out = lax.optimization_barrier((exchanged(second_out, "dp", 1), home_out))
+        second = exchanged((second + got.astype(f32) + relayed).astype(bf16), "seq", 2)
+        near = exchanged((near + exchanged(near_out, "dp", 1).astype(f32)).astype(bf16), "seq", 1)
+        home = home + exchanged(home_out, "dp", 1).astype(f32)
         home, grid = lax.optimization_barrier((home, grid))
-        summed = home + far.astype(f32) + second.astype(f32) + near.astype(f32)
+        summed = home + second.astype(f32) + near.astype(f32)
+    else:
+        partial = jnp.dot(rows_t, slope_grad, preferred_element_type=f32)
+        summed = lax.psum_scatter(partial, ("seq", "dp"), scatter_dimension=0, tiled=True)
     return (grid.reshape(1, frames_dev, patches, half), summed * norm_scale)
 
 

time: 64.4 us -> 61.5 us (0.955)
  starting transfers between devices: 23.6 us -> 22 us
  waiting for transfers between devices: 20.2 us -> 19 us
  local copies, waits for them, and re-layouts: 5.95 us -> 4.94 us
  Pallas kernels: 12.5 us -> 13.3 us
    ppermute x11, starting transfers between devices: 23.6 us -> 22 us  [exchanged(): lax.ppermute(array, axis, [(i, i ^ distance) for i in range(lax.axis_size...]
    ppermute x11, waiting for transfers between devices: 20.2 us -> 19 us  [exchanged(): lax.ppermute(array, axis, [(i, i ^ distance) for i in range(lax.axis_size...]
    pallas_call x1, Pallas kernels: 1.13 us -> 2.24 us  [shards(): call(functools.partial(pack_kernel, seq_size, frames_dev, slot_rows, part...]
    unnamed x12, local copies, waits for them, and re-layouts: 5.26 us -> 4.25 us
    pallas_call x4 -> x2, Pallas kernels: 4.45 us -> 4.16 us  [the longest x1 2.94 us: shards(): call(functools.partial(rest_kernel, chunks, tile), [shape(f32, slots, hal...]
  transfers between devices with their start and end apart: 11 -> 11, of which waited for: 4 -> 6; matrix products, arithmetic and copies ran while one was open for 1% -> 2% of each run, Pallas kernels for 17% -> 16%
where the time goes in v3:
time: 61.5 us; the launch traced here: 61.2 us
  starting transfers between devices  22 us (36%)
  waiting for transfers between devices  19 us (31%)
  Pallas kernels  13.3 us (22%)
  local copies, waits for them, and re-layouts  4.94 us (8%)
  other arithmetic  1.16 us (2%)
  between operations  0.71 us (1%)
    ppermute x11, starting transfers between devices, exchanged(): lax.ppermute(array, axis, [(i, i ^ distance) for i in range(lax.axis_size...  22 us
    ppermute x11, waiting for transfers between devices, exchanged(): lax.ppermute(array, axis, [(i, i ^ distance) for i in range(lax.axis_size...  19 us
    pallas_call x1, Pallas kernels, shards(): call(functools.partial(slope_kernel, seq_size, rows_dev, slot_rows, partn...  5.23 us
    unnamed x12, local copies, waits for them, and re-layouts  4.25 us
    pallas_call x1, Pallas kernels, shards(): call(functools.partial(rest_kernel, chunks, tile), [shape(f32, slots, hal...  2.94 us
    pallas_call x1, Pallas kernels, shards(): call(functools.partial(pack_kernel, seq_size, frames_dev, slot_rows, part...  2.24 us
    pallas_call x1, Pallas kernels, shards(): call(place_kernel, [shape(bf16, tokens, half)], [vmem] * 3, flops=2 * tok...  1.7 us
  transfers between devices with their start and end apart: 11, of which 6 were waited for; matrix products, arithmetic and copies ran while one was open for 2% of the time, Pallas kernels for 16%

profile of v3, /device:TPU:0, one launch (start us, length us, event | category | flops | bytes accessed | tf_op | source)
XLA Modules:
  0.0 61.2 jit_solution(5824976507466369800)
XLA Ops:
  0.6 2.2 %shard_map.78 = (bf16[144,896]{1,0:T(8,128)(2,1)}, bf16[144,896]{1,0:T(8,128)(2,1)}, bf16[144,896]{1,0:T(8,128)(2,1)}, bf16[144,896]{1,0:T(8,128)(2,1)}) custom-call(s32[1,16]{1,0:T(1,128)} %count_hbm.1, bf16[256,896]{1,0:T(8,128)(2,1)} %bitcast.7), custom_call_target="tpu_custom_call" | custom-call | flops 264241152 | bytes 1490944 | tf_op jit(solution)/shard_map/pallas_call | solution.py:179
  2.9 3.1 %collective-permute-start = (bf16[144,896]{1,0:T(8,128)(2,1)}, bf16[144,896]{1,0:T(8,128)(2,1)S(1)}, u32[]{:S(2)}, u32[]{:S(2)}) collective-permute-start(bf16[144,896]{1,0:T(8,128)(2,1)} %get-tuple-element.28), channel_id=1, source_target_pairs={{0,4},{4,0},{8,12},{12,8},{1,5},{5,1},{9,13},{13,9},{2,6},{6,2},{1... | collective-permute-start | bytes 774152 | tf_op jit(solution)/shard_map/ppermute | solution.py:36
  6.0 2.6 %collective-permute-start.1 = (bf16[144,896]{1,0:T(8,128)(2,1)}, bf16[144,896]{1,0:T(8,128)(2,1)S(1)}, u32[]{:S(2)}, u32[]{:S(2)}) collective-permute-start(bf16[144,896]{1,0:T(8,128)(2,1)} %get-tuple-element.29), channel_id=1, source_target_pairs={{0,8},{4,12},{8,0},{12,4},{1,9},{5,13},{9,1},{13,5},{2,10},{6,14},... | collective-permute-start | bytes 774152 | tf_op jit(solution)/shard_map/ppermute | solution.py:36
  8.6 0.0 collective-permute-start.2
  8.6 0.7 %reshape.21.bias_ref = f32[1,896]{1,0:T(1,128)S(1)} reshape(f32[896]{0:T(1024)} %param.9) | data formatting | bytes 7168 | tf_op jit(solution)/shard_map/reshape | solution.py:207
  9.2 0.0 copy-start.1
  9.2 1.6 %copy-done.1 = bf16[1152,896]{1,0:T(8,128)(2,1)S(1)} copy-done((bf16[1152,896]{1,0:T(8,128)(2,1)S(1)}, bf16[1152,896]{1,0:T(8,128)(2,1)}, u32[]{:S(2)}) %copy-start.1) | copy-done | bytes 2064408
  10.8 0.0 copy-start.3
  10.8 1.3 %copy-done.3 = bf16[1,4,144,1152]{3,2,1,0:T(8,128)(2,1)S(1)} copy-done((bf16[1,4,144,1152]{3,2,1,0:T(8,128)(2,1)S(1)}, bf16[1,4,144,1152]{3,2,1,0:T(8,128)(2,1)}, u32[]{:S(2)}) %copy-start.3) | copy-done | bytes 1327128
  12.1 0.0 copy-start.4
  12.2 0.7 %copy-done.4 = s32[1,4,144]{2,1,0:T(4,128)S(1)} copy-done((s32[1,4,144]{2,1,0:T(4,128)S(1)}, s32[1,4,144]{2,1,0:T(4,128)}, u32[]{:S(2)}) %copy-start.4) | copy-done | bytes 2328
  12.8 0.0 copy-start.5
  12.8 0.7 %copy-done.5 = s32[1,16]{1,0:T(1,128)S(1)} copy-done((s32[1,16]{1,0:T(1,128)S(1)}, s32[1,16]{1,0:T(1,128)}, u32[]{:S(2)}) %copy-start.5) | copy-done | bytes 88
  13.5 0.0 copy-start
  13.5 5.2 %shard_map.77 = (f32[576,896]{1,0:T(8,128)S(1)}, bf16[1152,576]{1,0:T(8,128)(2,1)S(1)}, bf16[576,576]{1,0:T(8,128)(2,1)S(1)}) custom-call(s32[1,16]{1,0:T(1,128)S(1)} %copy-done.5, s32[4,144]{1,0:T(4,128)S(1)} %bitcast.5, bf16[576,1152]{1,0:T(8,128)(2,1)S(1)} %bitcast.4, bf16[1152,896]{1,0:T(8,128)(2,1)S(1)} %copy-done.1, f32[1,896]{1,0:T(1,128)S(1)} %reshape.21.bias_ref), custom_call_target="tpu_custom_call" | custom-call | flops 1953497088 | bytes 6782976 | tf_op jit(solution)/shard_map/pallas_call | solution.py:199
  18.7 0.0 collective-permute-done.refs_1_
  18.7 8.5 %collective-permute-done.1.refs_2_ = bf16[144,896]{1,0:T(8,128)(2,1)S(1)} collective-permute-done((bf16[144,896]{1,0:T(8,128)(2,1)}, bf16[144,896]{1,0:T(8,128)(2,1)S(1)}, u32[]{:S(2)}, u32[]{:S(2)}) %collective-permute-start.1) | collective-permute-done | bytes 258080 | tf_op jit(solution)/shard_map/ppermute | solution.py:36
  27.3 0.0 collective-permute-done.2.refs_3_
  27.3 0.0 copy-done
  27.3 0.0 copy-start.2
  27.3 1.2 %shard_map.79 = (bf16[576,896]{1,0:T(8,128)(2,1)S(1)}, bf16[144,896]{1,0:T(8,128)(2,1)S(1)}, bf16[144,896]{1,0:T(8,128)(2,1)S(1)}, f32[144,896]{1,0:T(8,128)S(1)}, f32[144,896]{1,0:T(8,128)S(1)}) custom-call(bf16[144,896]{1,0:T(8,128)(2,1)S(1)} %copy-done, bf16[144,896]{1,0:T(8,128)(2,1)S(1)} %collective-permute-done.refs_1_, ...), custom_call_target="tpu_custom_call" | custom-call | flops 594542592 | bytes 5455872 | tf_op jit(solution)/shard_map/pallas_call | solution.py:218
  28.5 1.5 %collective-permute-start.6 = (bf16[144,896]{1,0:T(8,128)(2,1)S(1)}, bf16[144,896]{1,0:T(8,128)(2,1)S(1)}, u32[]{:S(2)}, u32[]{:S(2)}) collective-permute-start(bf16[144,896]{1,0:T(8,128)(2,1)S(1)} %get-tuple-element.45), channel_id=1, source_target_pairs={{0,2},{2,0},{1,3},{3,1},{4,6},{6,4},{5,7},{7,5},{8,10},{10,8},{9,1... | collective-permute-start | bytes 774152 | tf_op jit(solution)/shard_map/ppermute | solution.py:36
  30.1 0.5 collective-permute-start.3
  30.6 0.0 copy-done.2
  30.6 2.9 %shard_map.80 = (f32[576,576]{1,0:T(8,128)S(1)}, bf16[576,576]{1,0:T(8,128)(2,1)S(1)}, bf16[144,896]{1,0:T(8,128)(2,1)S(1)}, bf16[144,896]{1,0:T(8,128)(2,1)S(1)...) custom-call(bf16[1152,576]{1,0:T(8,128)(2,1)S(1)} %get-tuple-element.26.refs_5_.rows_t_ref, ...), custom_call_target="tpu_custom_call" | custom-call | flops 1783627776 | bytes 5087232 | tf_op jit(solution)/shard_map/pallas_call | solution.py:226
  33.6 3.3 %collective-permute-done.6 = bf16[144,896]{1,0:T(8,128)(2,1)S(1)} collective-permute-done((bf16[144,896]{1,0:T(8,128)(2,1)S(1)}, bf16[144,896]{1,0:T(8,128)(2,1)S(1)}, u32[]{:S(2)}, u32[]{:S(2)}) %collective-permute-start.6) | collective-permute-done | bytes 258080 | tf_op jit(solution)/shard_map/ppermute | solution.py:36
  36.8 0.1 add_convert_fusion.2
  36.9 5.6 %collective-permute-start.7 = (bf16[144,896]{1,0:T(8,128)(2,1)S(1)}, bf16[144,896]{1,0:T(8,128)(2,1)S(1)}, u32[]{:S(2)}, u32[]{:S(2)}) collective-permute-start(bf16[144,896]{1,0:T(8,128)(2,1)S(1)} %add_convert_fusion.2), channel_id=1, source_target_pairs={{0,4},{4,0},{8,12},{12,8},{1,5},{5,1},{9,13},{13,9},{2,6},{6,2},{1... | collective-permute-start | bytes 774152 | tf_op jit(solution)/shard_map/ppermute | solution.py:36
  42.5 1.5 %collective-permute-start.9 = (bf16[144,896]{1,0:T(8,128)(2,1)S(1)}, bf16[144,896]{1,0:T(8,128)(2,1)S(1)}, u32[]{:S(2)}, u32[]{:S(2)}) collective-permute-start(bf16[144,896]{1,0:T(8,128)(2,1)S(1)} %get-tuple-element.49), channel_id=1, source_target_pairs={{0,2},{2,0},{1,3},{3,1},{4,6},{6,4},{5,7},{7,5},{8,10},{10,8},{9,1... | collective-permute-start | bytes 774152 | tf_op jit(solution)/shard_map/ppermute | solution.py:36
  44.0 0.0 collective-permute-start.5
  44.0 0.0 collective-permute-done.3
  44.0 0.6 collective-permute-start.4
  44.6 2.3 %collective-permute-done.7 = bf16[144,896]{1,0:T(8,128)(2,1)S(1)} collective-permute-done((bf16[144,896]{1,0:T(8,128)(2,1)S(1)}, bf16[144,896]{1,0:T(8,128)(2,1)S(1)}, u32[]{:S(2)}, u32[]{:S(2)}) %collective-permute-start.7) | collective-permute-done | bytes 258080 | tf_op jit(solution)/shard_map/ppermute | solution.py:36
  46.8 0.1 add_convert_fusion.1
  46.9 4.1 %collective-permute-start.8 = (bf16[144,896]{1,0:T(8,128)(2,1)S(1)}, bf16[144,896]{1,0:T(8,128)(2,1)S(1)}, u32[]{:S(2)}, u32[]{:S(2)}) collective-permute-start(bf16[144,896]{1,0:T(8,128)(2,1)S(1)} %add_convert_fusion.1), channel_id=1, source_target_pairs={{0,8},{4,12},{8,0},{12,4},{1,9},{5,13},{9,1},{13,5},{2,10},{6,14},... | collective-permute-start | bytes 774152 | tf_op jit(solution)/shard_map/ppermute | solution.py:36
  51.0 0.0 collective-permute-done.9
  51.0 0.1 add_convert_fusion
  51.1 2.5 %collective-permute-start.10 = (bf16[144,896]{1,0:T(8,128)(2,1)S(1)}, bf16[144,896]{1,0:T(8,128)(2,1)S(1)}, u32[]{:S(2)}, u32[]{:S(2)}) collective-permute-start(bf16[144,896]{1,0:T(8,128)(2,1)S(1)} %add_convert_fusion), channel_id=1, source_target_pairs={{0,4},{4,0},{8,12},{12,8},{1,5},{5,1},{9,13},{13,9},{2,6},{6,2},{1... | collective-permute-start | bytes 774152 | tf_op jit(solution)/shard_map/ppermute | solution.py:36
  53.6 0.8 %collective-permute-done.4 = bf16[144,896]{1,0:T(8,128)(2,1)S(1)} collective-permute-done((bf16[144,896]{1,0:T(8,128)(2,1)S(1)}, bf16[144,896]{1,0:T(8,128)(2,1)S(1)}, u32[]{:S(2)}, u32[]{:S(2)}) %collective-permute-start.4) | collective-permute-done | bytes 258080 | tf_op jit(solution)/shard_map/ppermute | solution.py:36
  54.4 0.1 convert_add_fusion
  54.4 0.0 collective-permute-done.5.peer_ref
  54.5 1.7 %shard_map.81 = bf16[576,576]{1,0:T(8,128)(2,1)} custom-call(f32[576,576]{1,0:T(8,128)S(1)} %get-tuple-element.37.own_ref, bf16[576,576]{1,0:T(8,128)(2,1)S(1)} %collective-permute-done.5.peer_ref, bf16[576,576]{1,0:T(8,128)(2,1)S(1)} %get-tuple-element.39.place_ref), custom_call_target="tpu_custom_call" | custom-call | flops 382205952 | bytes 3981312 | tf_op jit(solution)/shard_map/pallas_call | solution.py:234
  56.2 3.5 %collective-permute-done.8 = bf16[144,896]{1,0:T(8,128)(2,1)S(1)} collective-permute-done((bf16[144,896]{1,0:T(8,128)(2,1)S(1)}, bf16[144,896]{1,0:T(8,128)(2,1)S(1)}, u32[]{:S(2)}, u32[]{:S(2)}) %collective-permute-start.8) | collective-permute-done | bytes 258080 | tf_op jit(solution)/shard_map/ppermute | solution.py:36
  59.6 0.7 %collective-permute-done.10 = bf16[144,896]{1,0:T(8,128)(2,1)S(1)} collective-permute-done((bf16[144,896]{1,0:T(8,128)(2,1)S(1)}, bf16[144,896]{1,0:T(8,128)(2,1)S(1)}, u32[]{:S(2)}, u32[]{:S(2)}) %collective-permute-start.10) | collective-permute-done | bytes 258080 | tf_op jit(solution)/shard_map/ppermute | solution.py:36
  60.3 0.9 %add_multiply_fusion = f32[144,896]{1,0:T(8,128)} fusion(bf16[144,896]{1,0:T(8,128)(2,1)S(1)} %collective-permute-done.10, f32[144,896]{1,0:T(8,128)S(1)} %convert_add_fusion, bf16[144,896]{1,0:T(8,128)(2,1)S(1)} %collective-permute-done.8), kind=kLoop, calls=%fused_computation | loop fusion | flops 645120 | bytes 1548288 | tf_op jit(solution)/shard_map/mul | solution.py:255
Async XLA Ops:
  2.9 15.9 %collective-permute-start = (bf16[144,896]{1,0:T(8,128)(2,1)}, bf16[144,896]{1,0:T(8,128)(2,1)S(1)}, u32[]{:S(2)}, u32[]{:S(2)}) collective-permute-start(bf16[144,896]{1,0:T(8,128)(2,1)} %get-tuple-element.28), channel_id=1, source_target_pairs={{0,4},{4,0},{8,12},{12,8},{1,5},{5,1},{9,13},{13,9},{2,6},{6,2},{1... | collective-permute-start | bytes 774152 | tf_op jit(solution)/shard_map/ppermute | solution.py:36
  6.0 21.3 %collective-permute-start.1 = (bf16[144,896]{1,0:T(8,128)(2,1)}, bf16[144,896]{1,0:T(8,128)(2,1)S(1)}, u32[]{:S(2)}, u32[]{:S(2)}) collective-permute-start(bf16[144,896]{1,0:T(8,128)(2,1)} %get-tuple-element.29), channel_id=1, source_target_pairs={{0,8},{4,12},{8,0},{12,4},{1,9},{5,13},{9,1},{13,5},{2,10},{6,14},... | collective-permute-start | bytes 774152 | tf_op jit(solution)/shard_map/ppermute | solution.py:36
  8.6 18.7 %collective-permute-start.2 = (bf16[144,896]{1,0:T(8,128)(2,1)}, bf16[144,896]{1,0:T(8,128)(2,1)S(1)}, u32[]{:S(2)}, u32[]{:S(2)}) collective-permute-start(bf16[144,896]{1,0:T(8,128)(2,1)} %get-tuple-element.30), channel_id=1, source_target_pairs={{0,12},{4,8},{8,4},{12,0},{1,13},{5,9},{9,5},{13,1},{2,14},{6,10},... | collective-permute-start | bytes 774152 | tf_op jit(solution)/shard_map/ppermute | solution.py:36
  9.2 1.6 %copy-start.1 = (bf16[1152,896]{1,0:T(8,128)(2,1)S(1)}, bf16[1152,896]{1,0:T(8,128)(2,1)}, u32[]{:S(2)}) copy-start(bf16[1152,896]{1,0:T(8,128)(2,1)} %weight_ref.3) | copy-start | bytes 6193156
  10.8 1.3 %copy-start.3 = (bf16[1,4,144,1152]{3,2,1,0:T(8,128)(2,1)S(1)}, bf16[1,4,144,1152]{3,2,1,0:T(8,128)(2,1)}, u32[]{:S(2)}) copy-start(bf16[1,4,144,1152]{3,2,1,0:T(8,128)(2,1)} %param.6) | copy-start | bytes 3981316
  12.1 0.7 %copy-start.4 = (s32[1,4,144]{2,1,0:T(4,128)S(1)}, s32[1,4,144]{2,1,0:T(4,128)}, u32[]{:S(2)}) copy-start(s32[1,4,144]{2,1,0:T(4,128)} %param.11) | copy-start | bytes 6916
  12.8 0.7 %copy-start.5 = (s32[1,16]{1,0:T(1,128)S(1)}, s32[1,16]{1,0:T(1,128)}, u32[]{:S(2)}) copy-start(s32[1,16]{1,0:T(1,128)} %count_hbm.1) | copy-start | bytes 196
  13.5 13.8 %copy-start = (bf16[144,896]{1,0:T(8,128)(2,1)S(1)}, bf16[144,896]{1,0:T(8,128)(2,1)}, u32[]{:S(2)}) copy-start(bf16[144,896]{1,0:T(8,128)(2,1)} %get-tuple-element.27.refs_0_) | copy-start | bytes 774148
  27.3 3.3 %copy-start.2 = (bf16[1152,896]{1,0:T(8,128)(2,1)S(1)}, bf16[1152,896]{1,0:T(8,128)(2,1)}, u32[]{:S(2)}) copy-start(bf16[1152,896]{1,0:T(8,128)(2,1)} %weight_ref.3) | copy-start | bytes 6193156
  28.5 8.3 %collective-permute-start.6 = (bf16[144,896]{1,0:T(8,128)(2,1)S(1)}, bf16[144,896]{1,0:T(8,128)(2,1)S(1)}, u32[]{:S(2)}, u32[]{:S(2)}) collective-permute-start(bf16[144,896]{1,0:T(8,128)(2,1)S(1)} %get-tuple-element.45), channel_id=1, source_target_pairs={{0,2},{2,0},{1,3},{3,1},{4,6},{6,4},{5,7},{7,5},{8,10},{10,8},{9,1... | collective-permute-start | bytes 774152 | tf_op jit(solution)/shard_map/ppermute | solution.py:36
  30.1 13.9 %collective-permute-start.3 = (bf16[144,896]{1,0:T(8,128)(2,1)S(1)}, bf16[144,896]{1,0:T(8,128)(2,1)S(1)}, u32[]{:S(2)}, u32[]{:S(2)}) collective-permute-start(bf16[144,896]{1,0:T(8,128)(2,1)S(1)} %get-tuple-element.34), channel_id=1, source_target_pairs={{0,2},{2,0},{1,3},{3,1},{4,6},{6,4},{5,7},{7,5},{8,10},{10,8},{9,1... | collective-permute-start | bytes 774152 | tf_op jit(solution)/shard_map/ppermute | solution.py:36
  36.9 9.9 %collective-permute-start.7 = (bf16[144,896]{1,0:T(8,128)(2,1)S(1)}, bf16[144,896]{1,0:T(8,128)(2,1)S(1)}, u32[]{:S(2)}, u32[]{:S(2)}) collective-permute-start(bf16[144,896]{1,0:T(8,128)(2,1)S(1)} %add_convert_fusion.2), channel_id=1, source_target_pairs={{0,4},{4,0},{8,12},{12,8},{1,5},{5,1},{9,13},{13,9},{2,6},{6,2},{1... | collective-permute-start | bytes 774152 | tf_op jit(solution)/shard_map/ppermute | solution.py:36
  42.5 8.5 %collective-permute-start.9 = (bf16[144,896]{1,0:T(8,128)(2,1)S(1)}, bf16[144,896]{1,0:T(8,128)(2,1)S(1)}, u32[]{:S(2)}, u32[]{:S(2)}) collective-permute-start(bf16[144,896]{1,0:T(8,128)(2,1)S(1)} %get-tuple-element.49), channel_id=1, source_target_pairs={{0,2},{2,0},{1,3},{3,1},{4,6},{6,4},{5,7},{7,5},{8,10},{10,8},{9,1... | collective-permute-start | bytes 774152 | tf_op jit(solution)/shard_map/ppermute | solution.py:36
  44.0 10.4 %collective-permute-start.5 = (bf16[576,576]{1,0:T(8,128)(2,1)S(1)}, bf16[576,576]{1,0:T(8,128)(2,1)S(1)}, u32[]{:S(2)}, u32[]{:S(2)}) collective-permute-start(bf16[576,576]{1,0:T(8,128)(2,1)S(1)} %get-tuple-element.38), channel_id=1, source_target_pairs={{0,1},{1,0},{2,3},{3,2},{4,5},{5,4},{6,7},{7,6},{8,9},{9,8},{10,11... | collective-permute-start | bytes 1990664 | tf_op jit(solution)/shard_map/ppermute | solution.py:36
  44.0 10.4 %collective-permute-start.4 = (bf16[144,896]{1,0:T(8,128)(2,1)S(1)}, bf16[144,896]{1,0:T(8,128)(2,1)S(1)}, u32[]{:S(2)}, u32[]{:S(2)}) collective-permute-start(bf16[144,896]{1,0:T(8,128)(2,1)S(1)} %get-tuple-element.36), channel_id=1, source_target_pairs={{0,2},{2,0},{1,3},{3,1},{4,6},{6,4},{5,7},{7,5},{8,10},{10,8},{9,1... | collective-permute-start | bytes 774152 | tf_op jit(solution)/shard_map/ppermute | solution.py:36
  46.9 12.7 %collective-permute-start.8 = (bf16[144,896]{1,0:T(8,128)(2,1)S(1)}, bf16[144,896]{1,0:T(8,128)(2,1)S(1)}, u32[]{:S(2)}, u32[]{:S(2)}) collective-permute-start(bf16[144,896]{1,0:T(8,128)(2,1)S(1)} %add_convert_fusion.1), channel_id=1, source_target_pairs={{0,8},{4,12},{8,0},{12,4},{1,9},{5,13},{9,1},{13,5},{2,10},{6,14},... | collective-permute-start | bytes 774152 | tf_op jit(solution)/shard_map/ppermute | solution.py:36
  51.1 9.2 %collective-permute-start.10 = (bf16[144,896]{1,0:T(8,128)(2,1)S(1)}, bf16[144,896]{1,0:T(8,128)(2,1)S(1)}, u32[]{:S(2)}, u32[]{:S(2)}) collective-permute-start(bf16[144,896]{1,0:T(8,128)(2,1)S(1)} %add_convert_fusion), channel_id=1, source_target_pairs={{0,4},{4,0},{8,12},{12,8},{1,5},{5,1},{9,13},{13,9},{2,6},{6,2},{1... | collective-permute-start | bytes 774152 | tf_op jit(solution)/shard_map/ppermute | solution.py:36

commit v4 on v3

--- a/solution.py
+++ b/solution.py
@@ -207,24 +207,24 @@
     )(keep_count, keep_order.reshape(frames_dev, patches), flat_tokens, weight, bias.reshape(1, hidden))
 
     half = width // lax.axis_size("mp")
-    early, late = ((3, 2), (1, 0)) if direct else ((), ())
-
-    def both(tiles):
-        chunks = [(k, j) for j in (1, 0) for k in tiles]
+    early = [(3, 1), (2, 1)] if direct else []
+    late = [(1, 1), (0, 1), (3, 0), (2, 0), (1, 0), (0, 0)] if direct else []
+
+    def tiles_of(chunks):
         outs = [shape(bf16 if j else f32, tile, hidden) for _, j in chunks]
-        return chunks, outs, 2 * sum(out.size for out in outs) * slots
-
-    chunks, outs, flops = both(early)
+        return outs, 2 * sum(out.size for out in outs) * slots
+
+    outs, flops = tiles_of(early)
     slope_grad, *first = call(
-        functools.partial(grad_kernel, len(arrived), chunks, tile),
+        functools.partial(grad_kernel, len(arrived), early, tile),
         [shape(bf16, slots, hidden), *outs],
         [vmem] * (len(arrived) + 2),
         flops=flops,
         moved=8 * slots * hidden + 2 * slots * width,
     )(*arrived, slope, rows_t)
-    chunks, outs, flops = both(late)
+    outs, flops = tiles_of(late)
     own_part, peer_part, *rest = call(
-        functools.partial(rest_kernel, chunks, tile),
+        functools.partial(rest_kernel, late, tile),
         [shape(f32, slots, half), shape(bf16, slots, half), *outs],
         [vmem] * 3,
         flops=flops + 2 * slots * width * hidden,
@@ -239,8 +239,8 @@
         moved=2 * tokens * (slots + half) + 8 * slots * half,
     )(own_part, peer_part, place)
     if direct:
-        far_out, second_out, far, second = first
-        near_out, home_out, near, home = rest
+        far_out, second_out = first
+        near_out, home_out, far, second, near, home = rest
         got, near_out = lax.optimization_barrier((exchanged(far_out, "dp", 1), near_out))
         relayed = exchanged((far + got.astype(f32)).astype(bf16), "seq", 1).astype(f32)
         got, home_out = lax.optimization_barrier((exchanged(second_out, "dp", 1), home_out))

time: 61.5 us -> 61 us (level)
  transfers between devices with their start and end apart: 11 -> 11, of which waited for: 6 -> 6; matrix products, arithmetic and copies ran while one was open for 2% -> 2% of each run, Pallas kernels for 16% -> 17%
where the time goes in v4:
time: 61 us; the launch traced here: 60.7 us
  starting transfers between devices  22 us (36%)
  waiting for transfers between devices  18.6 us (30%)
  Pallas kernels  13.3 us (22%)
  local copies, waits for them, and re-layouts  4.94 us (8%)
  other arithmetic  1.15 us (2%)
  between operations  0.71 us (1%)
    ppermute x11, starting transfers between devices, exchanged(): lax.ppermute(array, axis, [(i, i ^ distance) for i in range(lax.axis_size...  22 us
    ppermute x11, waiting for transfers between devices, exchanged(): lax.ppermute(array, axis, [(i, i ^ distance) for i in range(lax.axis_size...  18.6 us
    pallas_call x1, Pallas kernels, shards(): call(functools.partial(slope_kernel, seq_size, rows_dev, slot_rows, partn...  5.23 us
    unnamed x12, local copies, waits for them, and re-layouts  4.25 us
    pallas_call x1, Pallas kernels, shards(): call(functools.partial(rest_kernel, late, tile), [shape(f32, slots, half)...  3.4 us
    pallas_call x1, Pallas kernels, shards(): call(functools.partial(pack_kernel, seq_size, frames_dev, slot_rows, part...  2.24 us
    pallas_call x1, Pallas kernels, shards(): call(place_kernel, [shape(bf16, tokens, half)], [vmem] * 3, flops=2 * tok...  1.7 us
  transfers between devices with their start and end apart: 11, of which 6 were waited for; matrix products, arithmetic and copies ran while one was open for 2% of the time, Pallas kernels for 17%

profile of v4, /device:TPU:0, one launch (start us, length us, event | category | flops | bytes accessed | tf_op | source)
XLA Modules:
  0.0 60.7 jit_solution(836924441203594773)
XLA Ops:
  0.6 2.2 %shard_map.78 = (bf16[144,896]{1,0:T(8,128)(2,1)}, bf16[144,896]{1,0:T(8,128)(2,1)}, bf16[144,896]{1,0:T(8,128)(2,1)}, bf16[144,896]{1,0:T(8,128)(2,1)}) custom-call(s32[1,16]{1,0:T(1,128)} %count_hbm.1, bf16[256,896]{1,0:T(8,128)(2,1)} %bitcast.7), custom_call_target="tpu_custom_call" | custom-call | flops 264241152 | bytes 1490944 | tf_op jit(solution)/shard_map/pallas_call | solution.py:179
  2.9 3.1 %collective-permute-start = (bf16[144,896]{1,0:T(8,128)(2,1)}, bf16[144,896]{1,0:T(8,128)(2,1)S(1)}, u32[]{:S(2)}, u32[]{:S(2)}) collective-permute-start(bf16[144,896]{1,0:T(8,128)(2,1)} %get-tuple-element.28), channel_id=1, source_target_pairs={{0,4},{4,0},{8,12},{12,8},{1,5},{5,1},{9,13},{13,9},{2,6},{6,2},{1... | collective-permute-start | bytes 774152 | tf_op jit(solution)/shard_map/ppermute | solution.py:36
  6.0 2.6 %collective-permute-start.1 = (bf16[144,896]{1,0:T(8,128)(2,1)}, bf16[144,896]{1,0:T(8,128)(2,1)S(1)}, u32[]{:S(2)}, u32[]{:S(2)}) collective-permute-start(bf16[144,896]{1,0:T(8,128)(2,1)} %get-tuple-element.29), channel_id=1, source_target_pairs={{0,8},{4,12},{8,0},{12,4},{1,9},{5,13},{9,1},{13,5},{2,10},{6,14},... | collective-permute-start | bytes 774152 | tf_op jit(solution)/shard_map/ppermute | solution.py:36
  8.6 0.0 collective-permute-start.2
  8.6 0.7 %reshape.21.bias_ref = f32[1,896]{1,0:T(1,128)S(1)} reshape(f32[896]{0:T(1024)} %param.9) | data formatting | bytes 7168 | tf_op jit(solution)/shard_map/reshape | solution.py:207
  9.2 0.0 copy-start.1
  9.2 1.6 %copy-done.1 = bf16[1152,896]{1,0:T(8,128)(2,1)S(1)} copy-done((bf16[1152,896]{1,0:T(8,128)(2,1)S(1)}, bf16[1152,896]{1,0:T(8,128)(2,1)}, u32[]{:S(2)}) %copy-start.1) | copy-done | bytes 2064408
  10.8 0.0 copy-start.3
  10.8 1.3 %copy-done.3 = bf16[1,4,144,1152]{3,2,1,0:T(8,128)(2,1)S(1)} copy-done((bf16[1,4,144,1152]{3,2,1,0:T(8,128)(2,1)S(1)}, bf16[1,4,144,1152]{3,2,1,0:T(8,128)(2,1)}, u32[]{:S(2)}) %copy-start.3) | copy-done | bytes 1327128
  12.1 0.0 copy-start.4
  12.2 0.7 %copy-done.4 = s32[1,4,144]{2,1,0:T(4,128)S(1)} copy-done((s32[1,4,144]{2,1,0:T(4,128)S(1)}, s32[1,4,144]{2,1,0:T(4,128)}, u32[]{:S(2)}) %copy-start.4) | copy-done | bytes 2328
  12.8 0.0 copy-start.5
  12.8 0.7 %copy-done.5 = s32[1,16]{1,0:T(1,128)S(1)} copy-done((s32[1,16]{1,0:T(1,128)S(1)}, s32[1,16]{1,0:T(1,128)}, u32[]{:S(2)}) %copy-start.5) | copy-done | bytes 88
  13.5 0.0 copy-start
  13.5 5.2 %shard_map.77 = (f32[576,896]{1,0:T(8,128)S(1)}, bf16[1152,576]{1,0:T(8,128)(2,1)S(1)}, bf16[576,576]{1,0:T(8,128)(2,1)S(1)}) custom-call(s32[1,16]{1,0:T(1,128)S(1)} %copy-done.5, s32[4,144]{1,0:T(4,128)S(1)} %bitcast.5, bf16[576,1152]{1,0:T(8,128)(2,1)S(1)} %bitcast.4, bf16[1152,896]{1,0:T(8,128)(2,1)S(1)} %copy-done.1, f32[1,896]{1,0:T(1,128)S(1)} %reshape.21.bias_ref), custom_call_target="tpu_custom_call" | custom-call | flops 1953497088 | bytes 6782976 | tf_op jit(solution)/shard_map/pallas_call | solution.py:199
  18.7 0.0 collective-permute-done.refs_1_
  18.7 8.5 %collective-permute-done.1.refs_2_ = bf16[144,896]{1,0:T(8,128)(2,1)S(1)} collective-permute-done((bf16[144,896]{1,0:T(8,128)(2,1)}, bf16[144,896]{1,0:T(8,128)(2,1)S(1)}, u32[]{:S(2)}, u32[]{:S(2)}) %collective-permute-start.1) | collective-permute-done | bytes 258080 | tf_op jit(solution)/shard_map/ppermute | solution.py:36
  27.3 0.0 collective-permute-done.2.refs_3_
  27.3 0.0 copy-done
  27.3 0.0 copy-start.2
  27.3 0.8 %shard_map.79 = (bf16[576,896]{1,0:T(8,128)(2,1)S(1)}, bf16[144,896]{1,0:T(8,128)(2,1)S(1)}, bf16[144,896]{1,0:T(8,128)(2,1)S(1)}) custom-call(bf16[144,896]{1,0:T(8,128)(2,1)S(1)} %copy-done, bf16[144,896]{1,0:T(8,128)(2,1)S(1)} %collective-permute-done.refs_1_, bf16[144,896]{1,0:T(8,128)(2,1)S(1)} %collective-permute-done.1.refs_2_, ...), custom_call_target="tpu_custom_call" | custom-call | flops 297271296 | bytes 5455872 | tf_op jit(solution)/shard_map/pallas_call | solution.py:218
  28.0 1.5 %collective-permute-start.6 = (bf16[144,896]{1,0:T(8,128)(2,1)S(1)}, bf16[144,896]{1,0:T(8,128)(2,1)S(1)}, u32[]{:S(2)}, u32[]{:S(2)}) collective-permute-start(bf16[144,896]{1,0:T(8,128)(2,1)S(1)} %get-tuple-element.45), channel_id=1, source_target_pairs={{0,2},{2,0},{1,3},{3,1},{4,6},{6,4},{5,7},{7,5},{8,10},{10,8},{9,1... | collective-permute-start | bytes 774152 | tf_op jit(solution)/shard_map/ppermute | solution.py:36
  29.6 0.6 collective-permute-start.3
  30.1 0.0 copy-done.2
  30.1 3.4 %shard_map.80 = (f32[576,576]{1,0:T(8,128)S(1)}, bf16[576,576]{1,0:T(8,128)(2,1)S(1)}, bf16[144,896]{1,0:T(8,128)(2,1)S(1)}, bf16[144,896]{1,0:T(8,128)(2,1)S(1)...) custom-call(bf16[1152,576]{1,0:T(8,128)(2,1)S(1)} %get-tuple-element.26.ref, ...), custom_call_target="tpu_custom_call" | custom-call | flops 2080899072 | bytes 5087232 | tf_op jit(solution)/shard_map/pallas_call | solution.py:226
  33.5 2.8 %collective-permute-done.6 = bf16[144,896]{1,0:T(8,128)(2,1)S(1)} collective-permute-done((bf16[144,896]{1,0:T(8,128)(2,1)S(1)}, bf16[144,896]{1,0:T(8,128)(2,1)S(1)}, u32[]{:S(2)}, u32[]{:S(2)}) %collective-permute-start.6) | collective-permute-done | bytes 258080 | tf_op jit(solution)/shard_map/ppermute | solution.py:36
  36.4 0.1 add_convert_fusion.2
  36.4 5.6 %collective-permute-start.7 = (bf16[144,896]{1,0:T(8,128)(2,1)S(1)}, bf16[144,896]{1,0:T(8,128)(2,1)S(1)}, u32[]{:S(2)}, u32[]{:S(2)}) collective-permute-start(bf16[144,896]{1,0:T(8,128)(2,1)S(1)} %add_convert_fusion.2), channel_id=1, source_target_pairs={{0,4},{4,0},{8,12},{12,8},{1,5},{5,1},{9,13},{13,9},{2,6},{6,2},{1... | collective-permute-start | bytes 774152 | tf_op jit(solution)/shard_map/ppermute | solution.py:36
  42.1 1.5 %collective-permute-start.9 = (bf16[144,896]{1,0:T(8,128)(2,1)S(1)}, bf16[144,896]{1,0:T(8,128)(2,1)S(1)}, u32[]{:S(2)}, u32[]{:S(2)}) collective-permute-start(bf16[144,896]{1,0:T(8,128)(2,1)S(1)} %get-tuple-element.49), channel_id=1, source_target_pairs={{0,2},{2,0},{1,3},{3,1},{4,6},{6,4},{5,7},{7,5},{8,10},{10,8},{9,1... | collective-permute-start | bytes 774152 | tf_op jit(solution)/shard_map/ppermute | solution.py:36
  43.5 0.0 collective-permute-start.5
  43.5 0.0 collective-permute-done.3
  43.5 0.6 collective-permute-start.4
  44.1 2.3 %collective-permute-done.7 = bf16[144,896]{1,0:T(8,128)(2,1)S(1)} collective-permute-done((bf16[144,896]{1,0:T(8,128)(2,1)S(1)}, bf16[144,896]{1,0:T(8,128)(2,1)S(1)}, u32[]{:S(2)}, u32[]{:S(2)}) %collective-permute-start.7) | collective-permute-done | bytes 258080 | tf_op jit(solution)/shard_map/ppermute | solution.py:36
  46.4 0.1 add_convert_fusion.1
  46.5 4.0 %collective-permute-start.8 = (bf16[144,896]{1,0:T(8,128)(2,1)S(1)}, bf16[144,896]{1,0:T(8,128)(2,1)S(1)}, u32[]{:S(2)}, u32[]{:S(2)}) collective-permute-start(bf16[144,896]{1,0:T(8,128)(2,1)S(1)} %add_convert_fusion.1), channel_id=1, source_target_pairs={{0,8},{4,12},{8,0},{12,4},{1,9},{5,13},{9,1},{13,5},{2,10},{6,14},... | collective-permute-start | bytes 774152 | tf_op jit(solution)/shard_map/ppermute | solution.py:36
  50.5 0.0 collective-permute-done.9
  50.6 2.5 %collective-permute-start.10 = (bf16[144,896]{1,0:T(8,128)(2,1)S(1)}, bf16[144,896]{1,0:T(8,128)(2,1)S(1)}, u32[]{:S(2)}, u32[]{:S(2)}) collective-permute-start(bf16[144,896]{1,0:T(8,128)(2,1)S(1)} %add_convert_fusion), channel_id=1, source_target_pairs={{0,4},{4,0},{8,12},{12,8},{1,5},{5,1},{9,13},{13,9},{2,6},{6,2},{1... | collective-permute-start | bytes 774152 | tf_op jit(solution)/shard_map/ppermute | solution.py:36
  53.1 0.8 %collective-permute-done.4 = bf16[144,896]{1,0:T(8,128)(2,1)S(1)} collective-permute-done((bf16[144,896]{1,0:T(8,128)(2,1)S(1)}, bf16[144,896]{1,0:T(8,128)(2,1)S(1)}, u32[]{:S(2)}, u32[]{:S(2)}) %collective-permute-start.4) | collective-permute-done | bytes 258080 | tf_op jit(solution)/shard_map/ppermute | solution.py:36
  53.9 0.1 convert_add_fusion
  54.0 0.0 collective-permute-done.5.peer_ref
  54.0 1.7 %shard_map.81 = bf16[576,576]{1,0:T(8,128)(2,1)} custom-call(f32[576,576]{1,0:T(8,128)S(1)} %get-tuple-element.37.own_ref, bf16[576,576]{1,0:T(8,128)(2,1)S(1)} %collective-permute-done.5.peer_ref, bf16[576,576]{1,0:T(8,128)(2,1)S(1)} %get-tuple-element.39.place_ref), custom_call_target="tpu_custom_call" | custom-call | flops 382205952 | bytes 3981312 | tf_op jit(solution)/shard_map/pallas_call | solution.py:234
  55.7 3.5 %collective-permute-done.8 = bf16[144,896]{1,0:T(8,128)(2,1)S(1)} collective-permute-done((bf16[144,896]{1,0:T(8,128)(2,1)S(1)}, bf16[144,896]{1,0:T(8,128)(2,1)S(1)}, u32[]{:S(2)}, u32[]{:S(2)}) %collective-permute-start.8) | collective-permute-done | bytes 258080 | tf_op jit(solution)/shard_map/ppermute | solution.py:36
  59.1 0.7 %collective-permute-done.10 = bf16[144,896]{1,0:T(8,128)(2,1)S(1)} collective-permute-done((bf16[144,896]{1,0:T(8,128)(2,1)S(1)}, bf16[144,896]{1,0:T(8,128)(2,1)S(1)}, u32[]{:S(2)}, u32[]{:S(2)}) %collective-permute-start.10) | collective-permute-done | bytes 258080 | tf_op jit(solution)/shard_map/ppermute | solution.py:36
  59.8 0.9 %add_multiply_fusion = f32[144,896]{1,0:T(8,128)} fusion(bf16[144,896]{1,0:T(8,128)(2,1)S(1)} %collective-permute-done.10, f32[144,896]{1,0:T(8,128)S(1)} %convert_add_fusion, bf16[144,896]{1,0:T(8,128)(2,1)S(1)} %collective-permute-done.8), kind=kLoop, calls=%fused_computation | loop fusion | flops 645120 | bytes 1548288 | tf_op jit(solution)/shard_map/mul | solution.py:255
  (1 shorter events, 0.0 us)
Async XLA Ops:
  2.9 15.9 %collective-permute-start = (bf16[144,896]{1,0:T(8,128)(2,1)}, bf16[144,896]{1,0:T(8,128)(2,1)S(1)}, u32[]{:S(2)}, u32[]{:S(2)}) collective-permute-start(bf16[144,896]{1,0:T(8,128)(2,1)} %get-tuple-element.28), channel_id=1, source_target_pairs={{0,4},{4,0},{8,12},{12,8},{1,5},{5,1},{9,13},{13,9},{2,6},{6,2},{1... | collective-permute-start | bytes 774152 | tf_op jit(solution)/shard_map/ppermute | solution.py:36
  6.0 21.3 %collective-permute-start.1 = (bf16[144,896]{1,0:T(8,128)(2,1)}, bf16[144,896]{1,0:T(8,128)(2,1)S(1)}, u32[]{:S(2)}, u32[]{:S(2)}) collective-permute-start(bf16[144,896]{1,0:T(8,128)(2,1)} %get-tuple-element.29), channel_id=1, source_target_pairs={{0,8},{4,12},{8,0},{12,4},{1,9},{5,13},{9,1},{13,5},{2,10},{6,14},... | collective-permute-start | bytes 774152 | tf_op jit(solution)/shard_map/ppermute | solution.py:36
  8.6 18.7 %collective-permute-start.2 = (bf16[144,896]{1,0:T(8,128)(2,1)}, bf16[144,896]{1,0:T(8,128)(2,1)S(1)}, u32[]{:S(2)}, u32[]{:S(2)}) collective-permute-start(bf16[144,896]{1,0:T(8,128)(2,1)} %get-tuple-element.30), channel_id=1, source_target_pairs={{0,12},{4,8},{8,4},{12,0},{1,13},{5,9},{9,5},{13,1},{2,14},{6,10},... | collective-permute-start | bytes 774152 | tf_op jit(solution)/shard_map/ppermute | solution.py:36
  9.2 1.6 %copy-start.1 = (bf16[1152,896]{1,0:T(8,128)(2,1)S(1)}, bf16[1152,896]{1,0:T(8,128)(2,1)}, u32[]{:S(2)}) copy-start(bf16[1152,896]{1,0:T(8,128)(2,1)} %weight_ref.3) | copy-start | bytes 6193156
  10.8 1.3 %copy-start.3 = (bf16[1,4,144,1152]{3,2,1,0:T(8,128)(2,1)S(1)}, bf16[1,4,144,1152]{3,2,1,0:T(8,128)(2,1)}, u32[]{:S(2)}) copy-start(bf16[1,4,144,1152]{3,2,1,0:T(8,128)(2,1)} %param.6) | copy-start | bytes 3981316
  12.1 0.7 %copy-start.4 = (s32[1,4,144]{2,1,0:T(4,128)S(1)}, s32[1,4,144]{2,1,0:T(4,128)}, u32[]{:S(2)}) copy-start(s32[1,4,144]{2,1,0:T(4,128)} %param.11) | copy-start | bytes 6916
  12.8 0.7 %copy-start.5 = (s32[1,16]{1,0:T(1,128)S(1)}, s32[1,16]{1,0:T(1,128)}, u32[]{:S(2)}) copy-start(s32[1,16]{1,0:T(1,128)} %count_hbm.1) | copy-start | bytes 196
  13.5 13.8 %copy-start = (bf16[144,896]{1,0:T(8,128)(2,1)S(1)}, bf16[144,896]{1,0:T(8,128)(2,1)}, u32[]{:S(2)}) copy-start(bf16[144,896]{1,0:T(8,128)(2,1)} %get-tuple-element.27.refs_0_) | copy-start | bytes 774148
  27.3 2.9 %copy-start.2 = (bf16[1152,896]{1,0:T(8,128)(2,1)S(1)}, bf16[1152,896]{1,0:T(8,128)(2,1)}, u32[]{:S(2)}) copy-start(bf16[1152,896]{1,0:T(8,128)(2,1)} %weight_ref.3) | copy-start | bytes 6193156
  28.0 8.3 %collective-permute-start.6 = (bf16[144,896]{1,0:T(8,128)(2,1)S(1)}, bf16[144,896]{1,0:T(8,128)(2,1)S(1)}, u32[]{:S(2)}, u32[]{:S(2)}) collective-permute-start(bf16[144,896]{1,0:T(8,128)(2,1)S(1)} %get-tuple-element.45), channel_id=1, source_target_pairs={{0,2},{2,0},{1,3},{3,1},{4,6},{6,4},{5,7},{7,5},{8,10},{10,8},{9,1... | collective-permute-start | bytes 774152 | tf_op jit(solution)/shard_map/ppermute | solution.py:36
  29.6 13.9 %collective-permute-start.3 = (bf16[144,896]{1,0:T(8,128)(2,1)S(1)}, bf16[144,896]{1,0:T(8,128)(2,1)S(1)}, u32[]{:S(2)}, u32[]{:S(2)}) collective-permute-start(bf16[144,896]{1,0:T(8,128)(2,1)S(1)} %get-tuple-element.34), channel_id=1, source_target_pairs={{0,2},{2,0},{1,3},{3,1},{4,6},{6,4},{5,7},{7,5},{8,10},{10,8},{9,1... | collective-permute-start | bytes 774152 | tf_op jit(solution)/shard_map/ppermute | solution.py:36
  36.4 9.9 %collective-permute-start.7 = (bf16[144,896]{1,0:T(8,128)(2,1)S(1)}, bf16[144,896]{1,0:T(8,128)(2,1)S(1)}, u32[]{:S(2)}, u32[]{:S(2)}) collective-permute-start(bf16[144,896]{1,0:T(8,128)(2,1)S(1)} %add_convert_fusion.2), channel_id=1, source_target_pairs={{0,4},{4,0},{8,12},{12,8},{1,5},{5,1},{9,13},{13,9},{2,6},{6,2},{1... | collective-permute-start | bytes 774152 | tf_op jit(solution)/shard_map/ppermute | solution.py:36
  42.1 8.5 %collective-permute-start.9 = (bf16[144,896]{1,0:T(8,128)(2,1)S(1)}, bf16[144,896]{1,0:T(8,128)(2,1)S(1)}, u32[]{:S(2)}, u32[]{:S(2)}) collective-permute-start(bf16[144,896]{1,0:T(8,128)(2,1)S(1)} %get-tuple-element.49), channel_id=1, source_target_pairs={{0,2},{2,0},{1,3},{3,1},{4,6},{6,4},{5,7},{7,5},{8,10},{10,8},{9,1... | collective-permute-start | bytes 774152 | tf_op jit(solution)/shard_map/ppermute | solution.py:36
  43.5 10.4 %collective-permute-start.5 = (bf16[576,576]{1,0:T(8,128)(2,1)S(1)}, bf16[576,576]{1,0:T(8,128)(2,1)S(1)}, u32[]{:S(2)}, u32[]{:S(2)}) collective-permute-start(bf16[576,576]{1,0:T(8,128)(2,1)S(1)} %get-tuple-element.38), channel_id=1, source_target_pairs={{0,1},{1,0},{2,3},{3,2},{4,5},{5,4},{6,7},{7,6},{8,9},{9,8},{10,11... | collective-permute-start | bytes 1990664 | tf_op jit(solution)/shard_map/ppermute | solution.py:36
  43.5 10.4 %collective-permute-start.4 = (bf16[144,896]{1,0:T(8,128)(2,1)S(1)}, bf16[144,896]{1,0:T(8,128)(2,1)S(1)}, u32[]{:S(2)}, u32[]{:S(2)}) collective-permute-start(bf16[144,896]{1,0:T(8,128)(2,1)S(1)} %get-tuple-element.36), channel_id=1, source_target_pairs={{0,2},{2,0},{1,3},{3,1},{4,6},{6,4},{5,7},{7,5},{8,10},{10,8},{9,1... | collective-permute-start | bytes 774152 | tf_op jit(solution)/shard_map/ppermute | solution.py:36
  46.5 12.7 %collective-permute-start.8 = (bf16[144,896]{1,0:T(8,128)(2,1)S(1)}, bf16[144,896]{1,0:T(8,128)(2,1)S(1)}, u32[]{:S(2)}, u32[]{:S(2)}) collective-permute-start(bf16[144,896]{1,0:T(8,128)(2,1)S(1)} %add_convert_fusion.1), channel_id=1, source_target_pairs={{0,8},{4,12},{8,0},{12,4},{1,9},{5,13},{9,1},{13,5},{2,10},{6,14},... | collective-permute-start | bytes 774152 | tf_op jit(solution)/shard_map/ppermute | solution.py:36
  50.6 9.3 %collective-permute-start.10 = (bf16[144,896]{1,0:T(8,128)(2,1)S(1)}, bf16[144,896]{1,0:T(8,128)(2,1)S(1)}, u32[]{:S(2)}, u32[]{:S(2)}) collective-permute-start(bf16[144,896]{1,0:T(8,128)(2,1)S(1)} %add_convert_fusion), channel_id=1, source_target_pairs={{0,4},{4,0},{8,12},{12,8},{1,5},{5,1},{9,13},{13,9},{2,6},{6,2},{1... | collective-permute-start | bytes 774152 | tf_op jit(solution)/shard_map/ppermute | solution.py:36
